TPU v7x, 256 devices: a whole 4x4x8 slice. The times are simulated.
256 devices in a mesh: queue: 32 (over x_hi, z, core), mp: 8 (over x_lo, y).
Axes of the slice: x: 4 (x_hi: 2, x_lo: 2; x = x_hi * 2 + x_lo), y: 4, z: 8, core: 2. Of those that a mesh axis runs over, the one named last changes fastest.
Arguments:
- speech: bfloat16 [24576, 1024], P(('queue', 'mp')), may hold values from -6 to 6
- weight: bfloat16 [1024, 1024], P(None, 'mp'), may hold values from -0.1875 to 0.1875
- norm_gain: float32 [1024], replicated, may hold values from 0.1 to 1.9
- queue_keys: bfloat16 [24576, 1024], P('queue'), may hold values from -96 to 96
- new_keys: bfloat16 [768, 1024], replicated, may hold values from -6 to 6
- pointer: int32 [1], replicated, may hold values from 0 to 24575
- positives: int32 [24576], P(('queue', 'mp')), may hold values from 0 to 24575
Outputs:
- loss: float32 [24576], P(('queue', 'mp'))
- grad_speech: bfloat16 [24576, 1024], P(('queue', 'mp'))
- queue_next: bfloat16 [24576, 1024], P('queue')
All inputs are finite; a program needn't handle non-finite values.
Results may differ from a plain program's by a relative error of at most 0.022.
The roundings to bfloat16 on the way count: a program that leaves them out, or rounds other values in their place, can miss the bound.
Values may be sent and summed in bfloat16 or wider, within the bound.
No kernel may reach another device: no remote copies, remote signals or barrier semaphores. Data moves between devices by JAX's collectives and lax.ppermute only.
A program may use at most 128 MiB of HBM per device.

v0:
```python
import math

import jax
import jax.numpy as jnp
from jax import lax
from jax.sharding import PartitionSpec as P


def score_rows(all_queries, columns, key_rows, factor):
    total_rows = all_queries.shape[0]
    block_rows = math.gcd(total_rows, 512)
    block_count = total_rows // block_rows

    def score_block(pieces):
        query_block, column_block = pieces
        scores = (
            lax.dot_general(
                query_block, key_rows, (((1,), (1,)), ((), ())), preferred_element_type=jnp.float32
            )
            * factor
        )
        row_peak = jnp.max(scores, axis=1)
        row_total = jnp.sum(jnp.exp(scores - row_peak[:, None]), axis=1)
        is_positive = lax.broadcasted_iota(jnp.int32, scores.shape, 1) == column_block[:, None]
        row_positive = jnp.sum(jnp.where(is_positive, scores, 0.0), axis=1)
        return (scores, row_peak, row_total, row_positive)

    scores, row_peak, row_total, row_positive = lax.map(
        score_block,
        (
            all_queries.reshape(block_count, block_rows, -1),
            columns.reshape(block_count, block_rows),
        ),
    )
    return (
        scores.reshape(total_rows, -1),
        row_peak.reshape(-1),
        row_total.reshape(-1),
        row_positive.reshape(-1),
    )


def weighted_rows(scores, log_total, columns, key_rows):
    total_rows = scores.shape[0]
    block_rows = math.gcd(total_rows, 512)
    block_count = total_rows // block_rows

    def weight_block(pieces):
        score_block, total_block, column_block = pieces
        is_positive = lax.broadcasted_iota(jnp.int32, score_block.shape, 1) == column_block[:, None]
        weights = (
            jnp.exp(score_block - total_block[:, None]) - is_positive.astype(jnp.float32)
        ).astype(jnp.bfloat16)
        return jnp.dot(weights, key_rows, preferred_element_type=jnp.float32)

    result = lax.map(
        weight_block,
        (
            scores.reshape(block_count, block_rows, -1),
            log_total.reshape(block_count, block_rows),
            columns.reshape(block_count, block_rows),
        ),
    )
    return result.reshape(total_rows, key_rows.shape[1])


def shards(speech, weight, norm_gain, queue_keys, new_keys, pointer, positives):
    full_weight = lax.all_gather(weight, "mp", axis=1, tiled=True)
    hidden = jnp.dot(speech, full_weight, preferred_element_type=jnp.float32)
    inverse_rms = lax.rsqrt(jnp.mean(hidden * hidden, axis=1, keepdims=True) + 1e-06)
    queries = (hidden * inverse_rms * norm_gain).astype(jnp.bfloat16)
    all_queries, all_positives = (
        lax.all_gather(queries, "queue", axis=0, tiled=True),
        lax.all_gather(positives, "queue", axis=0, tiled=True),
    )
    key_count = queue_keys.shape[0]
    own_rows = speech.shape[0]
    width = queue_keys.shape[1]
    queue_index = lax.axis_index("queue")
    columns = all_positives - queue_index * key_count
    factor = 2.0 / math.sqrt(width)
    scores, row_peak, row_total, row_positive = score_rows(all_queries, columns, queue_keys, factor)
    global_peak = lax.pmax(row_peak, "queue")
    row_total, row_positive = lax.psum(
        (row_total * jnp.exp(row_peak - global_peak), row_positive), "queue"
    )
    row_peak = global_peak
    log_total = row_peak + jnp.log(row_total)
    losses = log_total - row_positive
    own_start = queue_index * own_rows
    loss_rows = lax.dynamic_slice_in_dim(losses, own_start, own_rows, 0)
    key_grad = lax.psum_scatter(
        weighted_rows(scores, log_total, columns, queue_keys).astype(jnp.bfloat16),
        "queue",
        scatter_dimension=0,
        tiled=True,
    ).astype(jnp.float32)
    key_grad = key_grad * (16.0 * factor)
    scaled = norm_gain * key_grad
    cubed = inverse_rms * inverse_rms * inverse_rms
    hidden_grad = (
        inverse_rms * scaled
        - hidden * cubed * jnp.sum(scaled * hidden, axis=1, keepdims=True) / width
    ).astype(jnp.bfloat16)
    grad_speech = lax.dot_general(
        hidden_grad, full_weight, (((1,), (1,)), ((), ())), preferred_element_type=jnp.float32
    ).astype(jnp.bfloat16)
    queue_length = key_count * lax.axis_size("queue")
    new_count = new_keys.shape[0]
    row_ids = queue_index * key_count + lax.broadcasted_iota(jnp.int32, (key_count,), 0)
    offsets = (row_ids - pointer[0]) % queue_length
    replaced = offsets < new_count
    taken = jnp.take(new_keys, jnp.minimum(offsets, new_count - 1), axis=0)
    queue_next = jnp.where(replaced[:, None], taken, queue_keys)
    return (loss_rows, grad_speech, queue_next)


def solution(mesh):
    return jax.shard_map(
        shards,
        mesh=mesh,
        in_specs=(
            P(("queue", "mp"), None),
            P(None, "mp"),
            P(),
            P("queue", None),
            P(),
            P(),
            P(("queue", "mp")),
        ),
        out_specs=(P(("queue", "mp")), P(("queue", "mp"), None), P("queue", None)),
        check_vma=False,
    )
```

profile of v0, /device:TPU:4, one launch (start us, length us, event | category | flops | bytes accessed | tf_op | source)
XLA Modules:
  0.0 682.7 jit_solution(9512552205144446500)
XLA Ops:
  7.2 0.7 all-gather.3.cloned.1.call-update
  8.0 52.1 %all-gather.3.cloned.1.call-done = bf16[1024,1024]{1,0:T(8,128)(2,1)} async-done(((bf16[1024,128]{1,0:T(8,128)(2,1)}), bf16[1024,1024]{1,0:T(8,128)(2,1)}) %all-gather.3.cloned.1.call-update) | async-done | bytes 2097168 | tf_op jit(solution)/shard_map/all_gather | solution.py:68
  60.1 2.3 multiply_reduce_fusion.1
  62.9 0.8 multiply_convert_fusion
  65.3 129.1 %all-reduce = s32[3072]{0:T(1024)S(1)} all-reduce(s32[3072]{0:T(1024)S(1)} %dynamic-update-slice), channel_id=1, replica_groups=mesh['queue'=32,'mp'=8] {'queue'}, use_global_device_ids=true, to_apply=%add | all-reduce | flops 3072 | bytes 24576
  195.1 56.5 %while.26 = (s32[]{:T(128)}, f32[6,512,768]{2,1,0:T(8,128)}, f32[6,512]{1,0:T(8,128)}, f32[6,512]{1,0:T(8,128)}, f32[6,512]{1,0:T(8,128)}, /*index=5*/bf16[6,512...) while((s32[]{:T(128)}, f32[6,512,768]{2,1,0:T(8,128)}, ...), condition=%wide.region_5.6_spmd, body=%wide.region_1.5_spmd.sunk | while | flops 808057344 | bytes 8940673 | solution.py:28
  195.1 3.9 bitcast_dynamic-update-slice_fusion.4
  199.2 0.7 constant_dynamic-slice_fusion.6
  199.9 0.6 select_reduce_fusion.2
  200.5 1.3 dynamic_update_slice.28
  201.8 1.3 dynamic_update_slice.27
  203.2 1.3 dynamic_update_slice.26
  204.5 3.9 bitcast_dynamic-update-slice_fusion.4
  208.6 0.7 constant_dynamic-slice_fusion.6
  209.3 0.6 select_reduce_fusion.2
  209.9 1.3 dynamic_update_slice.28
  211.3 1.3 dynamic_update_slice.27
  212.6 1.3 dynamic_update_slice.26
  213.9 3.9 bitcast_dynamic-update-slice_fusion.4
  218.0 0.7 constant_dynamic-slice_fusion.6
  218.7 0.6 select_reduce_fusion.2
  219.3 1.3 dynamic_update_slice.28
  220.6 1.3 dynamic_update_slice.27
  222.0 1.3 dynamic_update_slice.26
  223.3 3.9 bitcast_dynamic-update-slice_fusion.4
  227.4 0.7 constant_dynamic-slice_fusion.6
  228.1 0.6 select_reduce_fusion.2
  228.7 1.3 dynamic_update_slice.28
  230.1 1.3 dynamic_update_slice.27
  231.4 1.3 dynamic_update_slice.26
  232.7 3.9 bitcast_dynamic-update-slice_fusion.4
  236.8 0.7 constant_dynamic-slice_fusion.6
  238.1 1.3 dynamic_update_slice.28
  239.5 1.3 dynamic_update_slice.27
  240.8 1.3 dynamic_update_slice.26
  242.1 4.0 bitcast_dynamic-update-slice_fusion.4
  246.3 0.7 constant_dynamic-slice_fusion.6
  247.6 1.3 dynamic_update_slice.28
  249.0 1.3 dynamic_update_slice.27
  250.3 1.3 dynamic_update_slice.26
  251.6 0.7 reshape.100
  252.3 128.5 %pmax.7 = f32[3072]{0:T(1024)S(1)} all-reduce(f32[3072]{0:T(1024)S(1)} %reshape.100), channel_id=1, replica_groups=mesh['queue'=32,'mp'=8] {'queue'}, use_global_device_ids=true, to_apply=%region_6.7 | all-reduce | flops 3072 | bytes 24576 | tf_op jit(solution)/shard_map/pmax | solution.py:83
  380.9 0.7 reshape.101
  381.6 0.7 reshape.102
  382.3 129.2 %all-reduce.1 = (f32[3072]{0:T(1024)}, f32[3072]{0:T(1024)S(1)}) all-reduce(f32[3072]{0:T(1024)S(1)} %reshape.102, f32[3072]{0:T(1024)S(1)} %exponential_multiply_fusion), channel_id=1, replica_groups=mesh['queue'=32,'mp'=8] {'queue'}, use_global_device_ids=true, to_apply=%region_8.9 | all-reduce | flops 6144 | bytes 49152 | tf_op jit(solution)/shard_map/psum | solution.py:84
  511.5 28.4 %while.27 = (s32[]{:T(128)}, bf16[6,512,1024]{2,1,0:T(8,128)(2,1)}, f32[6,512,768]{2,1,0:T(8,128)}, f32[6,512]{1,0:T(8,128)S(1)}, s32[6,512]{1,0:T(8,128)}, /*index=5*/bf16[768,1024]{1,0:T(8,128)(2,1)}, s32[]{:T(128)}) while((s32[]{:T(128)}, bf16[6,512,1024]{2,1,0:T(8,128)(2,1)}, f32[6,512,768]{2,1,0:T(8,128)}, f32[6,512]{1,0:T(8,128)S(1)}, ...), condition=%wide.region_10.11_spmd, body=%wide.region_9.10_spmd.sunk | while | flops 807272448 | bytes 5256277 | solution.py:56
  511.5 0.7 constant_dynamic-slice_fusion.7
  512.2 4.0 bitcast_dynamic-update-slice_fusion.5
  516.2 0.7 constant_dynamic-slice_fusion.7
  516.9 4.0 bitcast_dynamic-update-slice_fusion.5
  520.9 0.7 constant_dynamic-slice_fusion.7
  521.7 4.0 bitcast_dynamic-update-slice_fusion.5
  525.6 0.7 constant_dynamic-slice_fusion.7
  526.4 4.1 bitcast_dynamic-update-slice_fusion.5
  530.4 0.7 constant_dynamic-slice_fusion.7
  531.2 4.0 bitcast_dynamic-update-slice_fusion.5
  535.1 0.7 constant_dynamic-slice_fusion.7
  535.9 4.0 bitcast_dynamic-update-slice_fusion.5
  541.2 3.8 gather_fusion
  545.0 2.9 select_select_fusion
  547.9 1.3 dynamic-slice_subtract_fusion
  549.2 122.7 %reduce-scatter.2.cloned.1.call-done = bf16[96,1024]{1,0:T(8,128)(2,1)} async-done(((bf16[3072,1024]{1,0:T(8,128)(2,1)}), bf16[96,1024]{1,0:T(8,128)(2,1)}) %reduce-scatter.2.cloned.1.call-update) | async-done | bytes 196624 | tf_op jit(solution)/shard_map/reduce_scatter | solution.py:92
  671.9 1.1 multiply_reduce_fusion
  673.0 3.2 convolution_convert_fusion
  (49 shorter events, 5.1 us)
Async XLA Ops:
  7.2 534.0 %copy-start = (bf16[768,1024]{1,0:T(8,128)(2,1)S(1)}, bf16[768,1024]{1,0:T(8,128)(2,1)}, u32[]{:S(2)}) copy-start(bf16[768,1024]{1,0:T(8,128)(2,1)} %param.15) | copy-start | bytes 4718596
  7.2 55.8 %copy-start.2 = (f32[1024]{0:T(1024)S(1)}, f32[1024]{0:T(1024)}, u32[]{:S(2)}) copy-start(f32[1024]{0:T(1024)} %param.13) | copy-start | bytes 12292
  7.2 52.9 %all-gather.3.cloned.1.call-start = ((), (), s32[]{:S(2)}) async-start(), calls=%async_computation.1 | async-start | bytes 2359296 | tf_op jit(solution)/shard_map/all_gather | solution.py:68
  7.9 55.9 %copy-start.5 = (u32[256]{0:T(256)S(1)}, u32[256]{0:T(256)}, u32[]{:S(2)}) copy-start(u32[256]{0:T(256)} %constant.90) | copy-start | bytes 3076
  7.9 57.1 %copy-start.4 = (s32[96]{0:T(128)S(1)}, s32[96]{0:T(128)}, u32[]{:S(2)}) copy-start(s32[96]{0:T(128)} %param.17) | copy-start | bytes 1156
  7.9 187.1 %all-gather.5.cloned.1.call-start = ((), (), s32[]{:S(2)}) async-start(), calls=%async_computation.2 | async-start | bytes 6488064 | tf_op jit(solution)/shard_map/all_gather | solution.py:73
  62.9 132.2 %copy-start.3 = (f32[96]{0:T(128)}, f32[96]{0:T(128)S(1)}, u32[]{:S(2)}) copy-start(f32[96]{0:T(128)S(1)} %get-tuple-element.120) | copy-start | bytes 1156
  63.7 608.2 %reduce-scatter.2.cloned.1.call-start = ((), (), s32[]{:S(2)}) async-start(), calls=%async_computation.3 | async-start | bytes 6488064 | tf_op jit(solution)/shard_map/reduce_scatter | solution.py:92
  541.2 3.8 copy-start.1
Sparse Core Ops, SparseCore 0:
  9.7 50.2 all-gather.2
  63.9 93.8 all-gather.4
  540.0 131.8 reduce-scatter.1
where the time goes:
time: 687 us; the launch traced here: 683 us
  blocking collectives  387 us (56%)
  waiting for transfers between devices  176 us (26%)
  matrix products  53 us (8%)
  local copies, waits for them, and re-layouts  40.2 us (6%)
  between operations  15.1 us (2%)
  other arithmetic  12 us (2%)
    psum x1, blocking collectives, shards(): lax.psum((row_total * jnp.exp(row_peak - global_peak), row_positive), 'qu...  129 us
    unnamed x1, blocking collectives  129 us
    pmax x1, blocking collectives, shards(): global_peak = lax.pmax(row_peak, 'queue')  129 us
    reduce_scatter x1, waiting for transfers between devices, shards(): lax.psum_scatter(weighted_rows(scores, log_total, columns, queue_keys).as...  123 us
    all_gather x1, waiting for transfers between devices, shards(): full_weight = lax.all_gather(weight, 'mp', axis=1, tiled=True)  52.1 us
    dot_general x6, matrix products, weight_block(): return jnp.dot(weights, key_rows, preferred_element_type=jnp.float32)  24 us
    dynamic_update_slice x18, local copies, waits for them, and re-layouts, score_rows(): lax.map(score_block, (all_queries.reshape(block_count, block_rows, -1), c...  23.9 us
    dot_general x6, matrix products, score_block(): lax.dot_general(query_block, key_rows, (((1,), (1,)), ((), ())), preferre...  23.5 us
  transfers between devices with their start and end apart: 3, of which 2 were waited for; matrix products, arithmetic and copies ran while one was open for 1% of the time, Pallas kernels for 0%

commit v1 on v0

v1 whole, which is shorter than its diff:
```python
import functools
import math

import jax
import jax.numpy as jnp
from jax import lax
from jax.experimental import pallas as pl
from jax.experimental.pallas import tpu as pltpu
from jax.sharding import PartitionSpec as P

RING = 8
BIG = 56 * 1024 * 1024
F32 = jnp.float32
BF16 = jnp.bfloat16
GATHER = (0, -1, 1, -2, 2, -3, 3, -4)
REDUCE = (4, -3, 3, -2, 2, -1, 1, 0)


def vmem():
    return pl.BlockSpec(memory_space=pltpu.VMEM)


def smem():
    return pl.BlockSpec(memory_space=pltpu.SMEM)


def queue_perm(move):
    def index(x, z, c):
        return (x * RING + z) * 2 + c

    return [
        (index(x, z, c), index(*move(x, z, c)))
        for x in range(2)
        for z in range(RING)
        for c in range(2)
    ]


UP = queue_perm(lambda x, z, c: (x, (z + 1) % RING, c))
DOWN = queue_perm(lambda x, z, c: (x, (z - 1) % RING, c))
CORE = queue_perm(lambda x, z, c: (x, z, 1 - c))
FAR = queue_perm(lambda x, z, c: (1 - x, z, c))


def score_kernel(factor, rows, place, *refs):
    slots = refs[:RING]
    weights = refs[RING : RING + 8]
    gain = refs[RING + 8]
    keys = refs[RING + 9 : RING + 13]
    probs, stats, wanted, own_hidden, full_weight = refs[RING + 13 : RING + 18]
    speech, hidden, queries, scores, table = refs[RING + 18 :]
    z, mp = place[0], place[1]
    width = hidden.shape[1]
    count = keys[0].shape[0]
    piece = weights[0].shape[1]

    for step in range(8):
        start = pl.multiple_of(jnp.bitwise_xor(mp, step) * piece, piece)
        full_weight[:, pl.ds(start, piece)] = weights[step][...]
    for slot, offset in enumerate(GATHER):
        owner = lax.rem(z + offset + RING, RING)
        start = pl.multiple_of(owner * rows, rows)
        speech[pl.ds(start, rows), :] = slots[slot][:, :width]
        codes = slots[slot][:, width:].astype(F32)
        ids = codes[:, 0:1] * 128.0 + codes[:, 1:2]
        wanted[pl.ds(start, rows), :] = jnp.broadcast_to(ids, (rows, 128))

    tile = 256

    @pl.loop(0, width // tile)
    def _(t):
        columns = pl.ds(pl.multiple_of(t * tile, tile), tile)
        hidden[:, columns] = jnp.dot(
            speech[...], full_weight[:, columns], preferred_element_type=F32
        )

    @pl.loop(0, RING)
    def _(b):
        span = pl.ds(pl.multiple_of(b * rows, rows), rows)
        block = hidden[span, :]
        inverse = lax.rsqrt(jnp.mean(block * block, axis=1, keepdims=True) + 1e-06)
        queries[span, :] = (block * inverse * gain[...]).astype(BF16)

    own_hidden[...] = hidden[pl.ds(pl.multiple_of(z * rows, rows), rows), :]

    for j in range(4):

        @pl.loop(0, count // tile)
        def _(t, j=j):
            key_rows = keys[j][pl.ds(pl.multiple_of(t * tile, tile), tile), :]
            product = lax.dot_general(
                queries[...], key_rows, (((1,), (1,)), ((), ())), preferred_element_type=F32
            )
            start = pl.multiple_of(j * count + t * tile, tile)
            scores[:, pl.ds(start, tile)] = product * factor

    step_rows = 32

    @pl.loop(0, RING * rows // step_rows)
    def _(b):
        span = pl.ds(pl.multiple_of(b * step_rows, step_rows), step_rows)
        block = scores[span, :]
        peak = jnp.max(block, axis=1, keepdims=True)
        powers = jnp.exp(block - peak)
        probs[span, :] = powers.astype(BF16)
        total = jnp.sum(powers, axis=1, keepdims=True)
        ids = wanted[span, :][:, 0:1].astype(jnp.int32)
        found = jnp.zeros((step_rows, 1), F32)
        for j in range(4):
            mine = lax.broadcasted_iota(jnp.int32, (step_rows, count), 1) == ids - place[2 + j]
            found += jnp.sum(
                jnp.where(mine, block[:, j * count : (j + 1) * count], 0.0), axis=1, keepdims=True
            )
        lane = lax.broadcasted_iota(jnp.int32, (step_rows, 128), 1)
        table[span, :] = jnp.where(
            lane == 0, peak, jnp.where(lane == 1, total, jnp.where(lane == 2, found, 0.0))
        )

    stats[...] = table[...].T[:8, :]


def product_kernel(place, probs, wanted, *refs):
    keys, (sums, picked) = refs[:4], refs[4:]
    count = keys[0].shape[0]
    ids = wanted[...][:, 0:1].astype(jnp.int32)
    total = jnp.zeros(sums.shape, F32)
    chosen = jnp.zeros(sums.shape, F32)
    for j in range(4):
        total += jnp.dot(
            probs[:, j * count : (j + 1) * count], keys[j][...], preferred_element_type=F32
        )
        mine = lax.broadcasted_iota(jnp.int32, (probs.shape[0], count), 1) == ids - place[2 + j]
        chosen += jnp.dot(
            mine.astype(F32).astype(BF16), keys[j][...], preferred_element_type=F32
        )
    sums[...] = total
    picked[...] = chosen.astype(BF16)


def scale_kernel(rows, place, sums, picked, local, merged, *refs):
    outs, loss, table = refs[:RING], refs[RING], refs[RING + 1]
    z = place[0]
    log_total = merged[0:1, :] + jnp.log(merged[1:2, :])
    scale = jnp.exp(local[0:1, :] - log_total)
    losses = log_total - merged[2:3, :]
    row = lax.broadcasted_iota(jnp.int32, (128, scale.shape[1]), 0)
    table[...] = jnp.where(row == 0, scale, jnp.where(row == 1, losses, 0.0)).T
    for slot, offset in enumerate(REDUCE):
        start = pl.multiple_of(lax.rem(z + offset + RING, RING) * rows, rows)
        span = pl.ds(start, rows)
        outs[slot][...] = (
            table[span, 0:1] * sums[span, :] - picked[span, :].astype(F32)
        ).astype(BF16)
    loss[...] = table[pl.ds(pl.multiple_of(z * rows, rows), rows), 1:2]


def final_kernel(factor, first, second, own, hidden, gain, weight, out):
    width = hidden.shape[1]
    grad = (first[...].astype(F32) + second[...].astype(F32) + own[...].astype(F32)) * factor
    scaled = gain[...] * grad
    values = hidden[...]
    inverse = lax.rsqrt(jnp.mean(values * values, axis=1, keepdims=True) + 1e-06)
    inner = jnp.sum(scaled * values, axis=1, keepdims=True)
    hidden_grad = (
        inverse * scaled - values * (inverse * inverse * inverse) * inner / width
    ).astype(BF16)
    out[...] = lax.dot_general(
        hidden_grad, weight[...], (((1,), (1,)), ((), ())), preferred_element_type=F32
    ).astype(BF16)


def queue_kernel(shift, keys, fresh, out):
    count = keys.shape[0]
    wanted = lax.broadcasted_iota(jnp.int32, (count, 1), 0) + shift[0]
    pick = lax.broadcasted_iota(jnp.int32, (count, fresh.shape[0]), 1) == wanted
    moved = jnp.dot(pick.astype(F32).astype(BF16), fresh[...], preferred_element_type=F32)
    replaced = (wanted >= 0) & (wanted < fresh.shape[0])
    out[...] = jnp.where(replaced, moved, keys[...].astype(F32)).astype(BF16)


def merge(mine, other):
    peak = jnp.maximum(mine[0:1], other[0:1])
    total = mine[1:2] * jnp.exp(mine[0:1] - peak) + other[1:2] * jnp.exp(other[0:1] - peak)
    found = mine[2:3] + other[2:3]
    row = lax.broadcasted_iota(jnp.int32, mine.shape, 0)
    return jnp.where(row == 0, peak, jnp.where(row == 1, total, found))


def shards(speech, weight, norm_gain, queue_keys, new_keys, pointer, positives):
    rows, width = speech.shape
    count = queue_keys.shape[0]
    total_rows = RING * rows
    queue_length = count * lax.axis_size("queue")
    queue_index = lax.axis_index("queue")
    mp = lax.axis_index("mp")
    z = (queue_index // 2) % RING
    factor = 2.0 / math.sqrt(width)
    params = pltpu.CompilerParams(vmem_limit_bytes=BIG)

    far = lax.ppermute(queue_keys, "queue", FAR)
    near = lax.ppermute(queue_keys, "queue", CORE)
    far_near = lax.ppermute(far, "queue", CORE)
    keys = (queue_keys, near, far, far_near)
    flipped = queue_index ^ (2 * RING)
    bases = [index * count for index in (queue_index, queue_index ^ 1, flipped, flipped ^ 1)]
    place = jnp.stack([z, mp] + bases).astype(jnp.int32)

    codes = jnp.stack([positives // 128, positives % 128], axis=1).astype(BF16)
    packed = jnp.concatenate([speech, jnp.pad(codes, ((0, 0), (0, 126)))], axis=1)
    slots = {0: packed}
    for step in range(1, 5):
        slots[-step] = lax.ppermute(slots[1 - step], "queue", UP)
        if step < 4:
            slots[step] = lax.ppermute(slots[step - 1], "queue", DOWN)
    pieces = [weight] + [
        lax.ppermute(weight, "mp", [(m, m ^ step) for m in range(8)]) for step in range(1, 8)
    ]
    gain = norm_gain.reshape(1, width)

    probs, stats, wanted, own_hidden, full_weight = pl.pallas_call(
        functools.partial(score_kernel, factor, rows),
        out_shape=(
            jax.ShapeDtypeStruct((total_rows, 4 * count), BF16),
            jax.ShapeDtypeStruct((8, total_rows), F32),
            jax.ShapeDtypeStruct((total_rows, 128), F32),
            jax.ShapeDtypeStruct((rows, width), F32),
            jax.ShapeDtypeStruct((width, width), BF16),
        ),
        in_specs=[smem()] + [vmem()] * (RING + 8 + 1 + 4),
        out_specs=(vmem(),) * 5,
        scratch_shapes=[
            pltpu.VMEM((total_rows, width), BF16),
            pltpu.VMEM((total_rows, width), F32),
            pltpu.VMEM((total_rows, width), BF16),
            pltpu.VMEM((total_rows, 4 * count), F32),
            pltpu.VMEM((total_rows, 128), F32),
        ],
        compiler_params=params,
        cost_estimate=pl.CostEstimate(
            flops=2 * total_rows * width * (4 * count + width),
            bytes_accessed=20_000_000,
            transcendentals=total_rows * 4 * count,
        ),
        name="scores",
    )(place, *[slots[offset] for offset in GATHER], *pieces, gain, *keys)

    merged = stats
    for step in (1, 2, 4):
        swap = queue_perm(lambda x, z, c, step=step: (x, z ^ step, c))
        merged = merge(merged, lax.ppermute(merged, "queue", swap))

    tile = 256
    sums, picked = pl.pallas_call(
        product_kernel,
        out_shape=(
            jax.ShapeDtypeStruct((total_rows, width), F32),
            jax.ShapeDtypeStruct((total_rows, width), BF16),
        ),
        grid=(width // tile,),
        in_specs=[
            smem(),
            pl.BlockSpec((total_rows, 4 * count), lambda t: (0, 0)),
            pl.BlockSpec((total_rows, 128), lambda t: (0, 0)),
        ]
        + [pl.BlockSpec((count, tile), lambda t: (0, t))] * 4,
        out_specs=(pl.BlockSpec((total_rows, tile), lambda t: (0, t)),) * 2,
        compiler_params=params,
        cost_estimate=pl.CostEstimate(
            flops=4 * total_rows * width * 4 * count, bytes_accessed=16_000_000, transcendentals=0
        ),
        name="products",
    )(place, probs, wanted, *keys)

    *grads, losses = pl.pallas_call(
        functools.partial(scale_kernel, rows),
        out_shape=[jax.ShapeDtypeStruct((rows, width), BF16)] * RING
        + [jax.ShapeDtypeStruct((rows, 1), F32)],
        in_specs=[smem()] + [vmem()] * 4,
        out_specs=[vmem()] * (RING + 1),
        scratch_shapes=[pltpu.VMEM((total_rows, 128), F32)],
        compiler_params=params,
        cost_estimate=pl.CostEstimate(
            flops=3 * total_rows * width, bytes_accessed=6_000_000, transcendentals=2000
        ),
        name="scaled",
    )(place, sums, picked, stats, merged)
    grads = dict(zip(REDUCE, grads))

    first, second = grads[4], grads[-3]
    for step in range(4):
        first = lax.ppermute(first, "queue", UP)
        if step < 3:
            first = (first.astype(F32) + grads[3 - step].astype(F32)).astype(BF16)
            second = lax.ppermute(second, "queue", DOWN)
            if step < 2:
                second = (second.astype(F32) + grads[step - 2].astype(F32)).astype(BF16)

    grad_speech = pl.pallas_call(
        functools.partial(final_kernel, 16.0 * factor),
        out_shape=jax.ShapeDtypeStruct((rows, width), BF16),
        in_specs=[vmem()] * 6,
        out_specs=vmem(),
        compiler_params=params,
        cost_estimate=pl.CostEstimate(
            flops=2 * rows * width * width, bytes_accessed=3_500_000, transcendentals=rows
        ),
        name="final",
    )(first, second, grads[0], own_hidden, gain, full_weight)

    shift = (queue_index * count - pointer) % queue_length
    shift = jnp.where(shift >= queue_length - count, shift - queue_length, shift)
    queue_next = pl.pallas_call(
        queue_kernel,
        out_shape=jax.ShapeDtypeStruct(queue_keys.shape, BF16),
        in_specs=[smem(), vmem(), vmem()],
        out_specs=vmem(),
        compiler_params=params,
        cost_estimate=pl.CostEstimate(
            flops=2 * count * count * width, bytes_accessed=5_000_000, transcendentals=0
        ),
        name="queue",
    )(shift, queue_keys, new_keys)
    return (losses.reshape(rows), grad_speech, queue_next)


def solution(mesh):
    return jax.shard_map(
        shards,
        mesh=mesh,
        in_specs=(
            P(("queue", "mp"), None),
            P(None, "mp"),
            P(),
            P("queue", None),
            P(),
            P(),
            P(("queue", "mp")),
        ),
        out_specs=(P(("queue", "mp")), P(("queue", "mp"), None), P("queue", None)),
        check_vma=False,
    )
```

time: 687 us -> 191 us (0.28)
  blocking collectives: 387 us -> 0 us
  waiting for transfers between devices: 176 us -> 85.7 us
  matrix products: 53 us -> 0 us
  Pallas kernels: 0 us -> 52.3 us
  starting transfers between devices: 0.12 us -> 41.4 us
  local copies, waits for them, and re-layouts: 40.2 us -> 2.65 us
  between operations: 15.1 us -> 1.51 us
    psum x1 -> x0, blocking collectives: 129 us -> none  [shards(): lax.psum((row_total * jnp.exp(row_peak - global_peak), row_positive), 'qu...]
    unnamed x1 -> x0, blocking collectives: 129 us -> none
    pmax x1 -> x0, blocking collectives: 129 us -> none  [shards(): global_peak = lax.pmax(row_peak, 'queue')]
    reduce_scatter x1 -> x0, waiting for transfers between devices: 123 us -> none  [shards(): lax.psum_scatter(weighted_rows(scores, log_total, columns, queue_keys).as...]
    ppermute x0 -> x27, waiting for transfers between devices: none -> 85.7 us  [the longest x1 35.6 us: shards(): far = lax.ppermute(queue_keys, 'queue', FAR)]
    dot_general x14 -> x0, matrix products: 53 us -> none  [the longest x6 24 us: weight_block(): return jnp.dot(weights, key_rows, preferred_element_type=jnp.float32)]
    pallas_call x0 -> x5, Pallas kernels: none -> 52.3 us  [the longest x1 25.6 us: shards(): pl.pallas_call(functools.partial(score_kernel, factor, rows), out_shape=(...]
    all_gather x2 -> x0, waiting for transfers between devices: 52.1 us -> none  [the longest x1 52.1 us: shards(): full_weight = lax.all_gather(weight, 'mp', axis=1, tiled=True)]
  transfers between devices with their start and end apart: 3 -> 27, of which waited for: 2 -> 15; matrix products, arithmetic and copies ran while one was open for 1% -> 3% of each run, Pallas kernels for 0% -> 10%
where the time goes in v1:
time: 191 us
  waiting for transfers between devices  85.7 us (45%)
  Pallas kernels  52.3 us (27%)
  starting transfers between devices  41.4 us (22%)
  other arithmetic  7.11 us (4%)
  local copies, waits for them, and re-layouts  2.65 us (1%)
    ppermute x1, waiting for transfers between devices, shards(): far = lax.ppermute(queue_keys, 'queue', FAR)  35.6 us
    pallas_call x1, Pallas kernels, shards(): pl.pallas_call(functools.partial(score_kernel, factor, rows), out_shape=(...  25.6 us
    ppermute x7, waiting for transfers between devices, shards(): lax.ppermute(weight, 'mp', [(m, m ^ step) for m in range(8)])  16.5 us
    pallas_call x1, Pallas kernels, shards(): pl.pallas_call(product_kernel, out_shape=(jax.ShapeDtypeStruct((total_row...  14.7 us
    ppermute x4, waiting for transfers between devices, shards(): first = lax.ppermute(first, 'queue', UP)  13.9 us
    ppermute x7, starting transfers between devices, shards(): lax.ppermute(weight, 'mp', [(m, m ^ step) for m in range(8)])  13.5 us
    ppermute x4, waiting for transfers between devices, shards(): slots[-step] = lax.ppermute(slots[1 - step], 'queue', UP)  10.8 us
    ppermute x3, starting transfers between devices, shards(): second = lax.ppermute(second, 'queue', DOWN)  9.91 us
  transfers between devices with their start and end apart: 27, of which 15 were waited for; matrix products, arithmetic and copies ran while one was open for 3% of the time, Pallas kernels for 10%

profile of v1, /device:TPU:4, one launch (start us, length us, event | category | flops | bytes accessed | tf_op | source)
XLA Modules:
  0.0 190.7 jit_solution(2538437693446093213)
XLA Ops:
  0.6 2.3 %collective-permute-start.15 = (bf16[768,1024]{1,0:T(8,128)(2,1)}, bf16[768,1024]{1,0:T(8,128)(2,1)S(1)}, u32[]{:S(2)}, u32[]{:S(2)}) collective-permute-start(bf16[768,1024]{1,0:T(8,128)(2,1)} %keys.1), channel_id=1, source_target_pairs={{0,128},{8,136},{16,144},{24,152},{32,160},{40,168},{48,176},{56,1... | collective-permute-start | bytes 4718600 | tf_op jit(solution)/shard_map/ppermute | solution.py:200
  3.0 0.0 collective-permute-start.14
  3.0 35.6 %collective-permute-done.15.refs_19_.refs_2_ = bf16[768,1024]{1,0:T(8,128)(2,1)S(1)} collective-permute-done((bf16[768,1024]{1,0:T(8,128)(2,1)}, bf16[768,1024]{1,0:T(8,128)(2,1)S(1)}, u32[]{:S(2)}, u32[]{:S(2)}) %collective-permute-start.15) | collective-permute-done | bytes 1572896 | tf_op jit(solution)/shard_map/ppermute | solution.py:200
  38.6 0.7 convert_bitcast_fusion
  39.3 0.1 copy.14
  39.4 0.9 fusion.1.refs_0_
  40.3 2.0 %collective-permute-start = (bf16[96,1152]{1,0:T(8,128)(2,1)S(1)}, bf16[96,1152]{1,0:T(8,128)(2,1)S(1)}, u32[]{:S(2)}, u32[]{:S(2)}) collective-permute-start(bf16[96,1152]{1,0:T(8,128)(2,1)S(1)} %fusion.1.refs_0_), channel_id=1, source_target_pairs={{0,16},{8,24},{16,32},{24,40},{32,48},{40,56},{48,64},{56,72},{64,... | collective-permute-start | bytes 663560 | tf_op jit(solution)/shard_map/ppermute | solution.py:212
  42.3 4.0 %collective-permute-start.1 = (bf16[96,1152]{1,0:T(8,128)(2,1)S(1)}, bf16[96,1152]{1,0:T(8,128)(2,1)S(1)}, u32[]{:S(2)}, u32[]{:S(2)}) collective-permute-start(bf16[96,1152]{1,0:T(8,128)(2,1)S(1)} %fusion.1.refs_0_), channel_id=1, source_target_pairs={{0,112},{8,120},{16,0},{24,8},{32,16},{40,24},{48,32},{56,40},{64,... | collective-permute-start | bytes 663560 | tf_op jit(solution)/shard_map/ppermute | solution.py:214
  46.4 1.6 collective-permute-start.7
  47.9 4.4 %collective-permute-done.refs_1_ = bf16[96,1152]{1,0:T(8,128)(2,1)S(1)} collective-permute-done((bf16[96,1152]{1,0:T(8,128)(2,1)S(1)}, bf16[96,1152]{1,0:T(8,128)(2,1)S(1)}, u32[]{:S(2)}, u32[]{:S(2)}) %collective-permute-start) | collective-permute-done | bytes 221216 | tf_op jit(solution)/shard_map/ppermute | solution.py:212
  52.4 3.2 %collective-permute-start.8 = (bf16[1024,128]{1,0:T(8,128)(2,1)}, bf16[1024,128]{1,0:T(8,128)(2,1)}, u32[]{:S(2)}, u32[]{:S(2)}) collective-permute-start(bf16[1024,128]{1,0:T(8,128)(2,1)} %refs_8_.1), channel_id=1, source_target_pairs={{0,2},{1,3},{2,0},{3,1},{4,6},{5,7},{6,4},{7,5},{8,10},{9,11},{10,... | collective-permute-start | bytes 786440 | tf_op jit(solution)/shard_map/ppermute | solution.py:216
  55.6 0.0 collective-permute-done.1.refs_2_
  55.6 1.1 collective-permute-start.9
  56.6 1.2 collective-permute-start.10
  57.8 5.5 %collective-permute-done.8.refs_10_ = bf16[1024,128]{1,0:T(8,128)(2,1)} collective-permute-done((bf16[1024,128]{1,0:T(8,128)(2,1)}, bf16[1024,128]{1,0:T(8,128)(2,1)}, u32[]{:S(2)}, u32[]{:S(2)}) %collective-permute-start.8) | collective-permute-done | bytes 262176 | tf_op jit(solution)/shard_map/ppermute | solution.py:216
  63.3 1.4 collective-permute-start.11
  64.6 4.2 %collective-permute-done.9.refs_11_ = bf16[1024,128]{1,0:T(8,128)(2,1)} collective-permute-done((bf16[1024,128]{1,0:T(8,128)(2,1)}, bf16[1024,128]{1,0:T(8,128)(2,1)}, u32[]{:S(2)}, u32[]{:S(2)}) %collective-permute-start.9) | collective-permute-done | bytes 262176 | tf_op jit(solution)/shard_map/ppermute | solution.py:216
  68.8 0.0 collective-permute-start.2
  68.8 2.3 %collective-permute-start.12 = (bf16[1024,128]{1,0:T(8,128)(2,1)}, bf16[1024,128]{1,0:T(8,128)(2,1)}, u32[]{:S(2)}, u32[]{:S(2)}) collective-permute-start(bf16[1024,128]{1,0:T(8,128)(2,1)} %refs_8_.1), channel_id=1, source_target_pairs={{0,6},{1,7},{2,4},{3,5},{4,2},{5,3},{6,0},{7,1},{8,14},{9,15},{10,... | collective-permute-start | bytes 786440 | tf_op jit(solution)/shard_map/ppermute | solution.py:216
  71.1 0.9 collective-permute-done.11.refs_13_
  72.1 2.2 %collective-permute-start.3 = (bf16[96,1152]{1,0:T(8,128)(2,1)S(1)}, bf16[96,1152]{1,0:T(8,128)(2,1)}, u32[]{:S(2)}, u32[]{:S(2)}) collective-permute-start(bf16[96,1152]{1,0:T(8,128)(2,1)S(1)} %collective-permute-done.1.refs_2_), channel_id=1, source_target_pairs={{0,112},{8,120},{16,0},{24,8},{32,16},{40,24},{48,32},{56,40},{64,... | collective-permute-start | bytes 663560 | tf_op jit(solution)/shard_map/ppermute | solution.py:214
  74.3 3.1 %collective-permute-done.2.refs_3_ = bf16[96,1152]{1,0:T(8,128)(2,1)S(1)} collective-permute-done((bf16[96,1152]{1,0:T(8,128)(2,1)S(1)}, bf16[96,1152]{1,0:T(8,128)(2,1)S(1)}, u32[]{:S(2)}, u32[]{:S(2)}) %collective-permute-start.2) | collective-permute-done | bytes 221216 | tf_op jit(solution)/shard_map/ppermute | solution.py:212
  77.4 2.5 %collective-permute-done.12.refs_14_ = bf16[1024,128]{1,0:T(8,128)(2,1)} collective-permute-done((bf16[1024,128]{1,0:T(8,128)(2,1)}, bf16[1024,128]{1,0:T(8,128)(2,1)}, u32[]{:S(2)}, u32[]{:S(2)}) %collective-permute-start.12) | collective-permute-done | bytes 262176 | tf_op jit(solution)/shard_map/ppermute | solution.py:216
  79.8 2.8 %collective-permute-start.13 = (bf16[1024,128]{1,0:T(8,128)(2,1)}, bf16[1024,128]{1,0:T(8,128)(2,1)}, u32[]{:S(2)}, u32[]{:S(2)}) collective-permute-start(bf16[1024,128]{1,0:T(8,128)(2,1)} %refs_8_.1), channel_id=1, source_target_pairs={{0,7},{1,6},{2,5},{3,4},{4,3},{5,2},{6,1},{7,0},{8,15},{9,14},{10,... | collective-permute-start | bytes 786440 | tf_op jit(solution)/shard_map/ppermute | solution.py:216
  82.6 0.0 collective-permute-done.3.refs_4_
  82.7 2.9 %collective-permute-start.5 = (bf16[96,1152]{1,0:T(8,128)(2,1)}, bf16[96,1152]{1,0:T(8,128)(2,1)}, u32[]{:S(2)}, u32[]{:S(2)}) collective-permute-start(bf16[96,1152]{1,0:T(8,128)(2,1)} %collective-permute-done.3.refs_4_), channel_id=1, source_target_pairs={{0,112},{8,120},{16,0},{24,8},{32,16},{40,24},{48,32},{56,40},{64,... | collective-permute-start | bytes 663560 | tf_op jit(solution)/shard_map/ppermute | solution.py:214
  85.5 0.0 collective-permute-done.4.refs_5_
  85.5 0.0 collective-permute-start.6
  85.5 0.7 stack.39.place
  86.2 3.4 %collective-permute-done.13.refs_15_ = bf16[1024,128]{1,0:T(8,128)(2,1)} collective-permute-done((bf16[1024,128]{1,0:T(8,128)(2,1)}, bf16[1024,128]{1,0:T(8,128)(2,1)}, u32[]{:S(2)}, u32[]{:S(2)}) %collective-permute-start.13) | collective-permute-done | bytes 262176 | tf_op jit(solution)/shard_map/ppermute | solution.py:216
  89.7 3.3 %collective-permute-done.6.refs_7_ = bf16[96,1152]{1,0:T(8,128)(2,1)} collective-permute-done((bf16[96,1152]{1,0:T(8,128)(2,1)}, bf16[96,1152]{1,0:T(8,128)(2,1)}, u32[]{:S(2)}, u32[]{:S(2)}) %collective-permute-start.6) | collective-permute-done | bytes 221216 | tf_op jit(solution)/shard_map/ppermute | solution.py:212
  93.0 1.1 copy-done.7
  94.1 25.6 %scores.1 = (bf16[768,3072]{1,0:T(8,128)(2,1)}, f32[8,768]{1,0:T(8,128)}, f32[768,128]{1,0:T(8,128)}, f32[96,1024]{1,0:T(8,128)}, bf16[1024,1024]{1,0:T(8,128)(2,1)}) custom-call(s32[6]{0:T(128)} %stack.39.place, bf16[96,1152]{1,0:T(8,128)(2,1)} %copy-done, bf16[96,1152]{1,0:T(8,128)(2,1)} %copy-done.8, bf16[96,1152]{1,0:T(8,128)(2,1)} %copy-done.9, ...), custom_call_target="tpu_custom_call" | custom-call | flops 6442450944 | bytes 20000000 | tf_op jit(solution)/shard_map/scores/pallas_call | solution.py:220
  119.7 0.1 collective-permute-start.17
  119.9 4.0 %collective-permute-done.17 = f32[8,768]{1,0:T(8,128)S(1)} collective-permute-done((f32[8,768]{1,0:T(8,128)}, f32[8,768]{1,0:T(8,128)S(1)}, u32[]{:S(2)}, u32[]{:S(2)}) %collective-permute-start.17) | collective-permute-done | bytes 24608 | tf_op jit(solution)/shard_map/ppermute | solution.py:250
  123.9 0.9 maximum_reduce_fusion.2
  124.8 0.1 select_select_fusion.2
  124.8 0.0 collective-permute-start.18
  124.9 4.9 %collective-permute-done.18 = f32[8,768]{1,0:T(8,128)S(1)} collective-permute-done((f32[8,768]{1,0:T(8,128)S(1)}, f32[8,768]{1,0:T(8,128)S(1)}, u32[]{:S(2)}, u32[]{:S(2)}) %collective-permute-start.18) | collective-permute-done | bytes 24608 | tf_op jit(solution)/shard_map/ppermute | solution.py:250
  129.8 0.1 select_select_fusion.1
  129.9 4.0 %collective-permute-start.19 = (f32[8,768]{1,0:T(8,128)S(1)}, f32[8,768]{1,0:T(8,128)S(1)}, u32[]{:S(2)}, u32[]{:S(2)}) collective-permute-start(f32[8,768]{1,0:T(8,128)S(1)} %select_select_fusion.1), channel_id=1, source_target_pairs={{0,64},{8,72},{16,80},{24,88},{32,96},{40,104},{48,112},{56,120},{... | collective-permute-start | bytes 73736 | tf_op jit(solution)/shard_map/ppermute | solution.py:250
  133.9 14.7 %products.1 = (f32[768,1024]{1,0:T(8,128)}, bf16[768,1024]{1,0:T(8,128)(2,1)}) custom-call(s32[6]{0:T(128)} %stack.39.place, bf16[768,3072]{1,0:T(8,128)(2,1)} %get-tuple-element.19.probs, f32[768,128]{1,0:T(8,128)} %get-tuple-element.20.wanted, bf16[768,1024]{1,0:T(8,128)(2,1)} %keys.1, bf16[768,1024]{1,0:T(8,128)(2,1)} %copy-done.7, ...), custom_call_target="tpu_custom_call" | custom-call | flops 9663676416 | bytes 16000000 | tf_op jit(solution)/shard_map/products/pallas_call | solution.py:253
  148.7 0.7 select_select_fusion.merged
  149.4 4.0 %scaled.1 = (bf16[96,1024]{1,0:T(8,128)(2,1)}, bf16[96,1024]{1,0:T(8,128)(2,1)}, bf16[96,1024]{1,0:T(8,128)(2,1)}, bf16[96,1024]{1,0:T(8,128)(2,1)}, bf16[96,102...) custom-call(s32[6]{0:T(128)} %stack.39.place, ...), custom_call_target="tpu_custom_call" | custom-call | flops 2359296 | bytes 6000000 | tf_op jit(solution)/shard_map/scaled/pallas_call | solution.py:274
  153.4 0.2 collective-permute-start.20
  153.6 3.1 %collective-permute-start.24 = (bf16[96,1024]{1,0:T(8,128)(2,1)}, bf16[96,1024]{1,0:T(8,128)(2,1)S(1)}, u32[]{:S(2)}, u32[]{:S(2)}) collective-permute-start(bf16[96,1024]{1,0:T(8,128)(2,1)} %get-tuple-element.29), channel_id=1, source_target_pairs={{0,112},{8,120},{16,0},{24,8},{32,16},{40,24},{48,32},{56,40},{64,... | collective-permute-start | bytes 589832 | tf_op jit(solution)/shard_map/ppermute | solution.py:294
  156.7 5.7 %collective-permute-done.20 = bf16[96,1024]{1,0:T(8,128)(2,1)S(1)} collective-permute-done((bf16[96,1024]{1,0:T(8,128)(2,1)}, bf16[96,1024]{1,0:T(8,128)(2,1)S(1)}, u32[]{:S(2)}, u32[]{:S(2)}) %collective-permute-start.20) | collective-permute-done | bytes 196640 | tf_op jit(solution)/shard_map/ppermute | solution.py:291
  162.3 1.0 add_convert_fusion.4
  163.3 0.1 collective-permute-start.21
  163.4 1.0 add_convert_fusion.1
  164.4 3.3 %collective-permute-start.25 = (bf16[96,1024]{1,0:T(8,128)(2,1)S(1)}, bf16[96,1024]{1,0:T(8,128)(2,1)S(1)}, u32[]{:S(2)}, u32[]{:S(2)}) collective-permute-start(bf16[96,1024]{1,0:T(8,128)(2,1)S(1)} %add_convert_fusion.1), channel_id=1, source_target_pairs={{0,112},{8,120},{16,0},{24,8},{32,16},{40,24},{48,32},{56,40},{64,... | collective-permute-start | bytes 589832 | tf_op jit(solution)/shard_map/ppermute | solution.py:294
  167.7 3.8 %collective-permute-done.21 = bf16[96,1024]{1,0:T(8,128)(2,1)S(1)} collective-permute-done((bf16[96,1024]{1,0:T(8,128)(2,1)S(1)}, bf16[96,1024]{1,0:T(8,128)(2,1)S(1)}, u32[]{:S(2)}, u32[]{:S(2)}) %collective-permute-start.21) | collective-permute-done | bytes 196640 | tf_op jit(solution)/shard_map/ppermute | solution.py:291
  171.5 1.0 add_convert_fusion.3
  172.5 0.1 collective-permute-start.22
  172.6 0.1 add_convert_fusion
  172.7 3.5 %collective-permute-start.26 = (bf16[96,1024]{1,0:T(8,128)(2,1)S(1)}, bf16[96,1024]{1,0:T(8,128)(2,1)S(1)}, u32[]{:S(2)}, u32[]{:S(2)}) collective-permute-start(bf16[96,1024]{1,0:T(8,128)(2,1)S(1)} %add_convert_fusion), channel_id=1, source_target_pairs={{0,112},{8,120},{16,0},{24,8},{32,16},{40,24},{48,32},{56,40},{64,... | collective-permute-start | bytes 589832 | tf_op jit(solution)/shard_map/ppermute | solution.py:294
  176.2 3.3 %collective-permute-done.22 = bf16[96,1024]{1,0:T(8,128)(2,1)S(1)} collective-permute-done((bf16[96,1024]{1,0:T(8,128)(2,1)S(1)}, bf16[96,1024]{1,0:T(8,128)(2,1)S(1)}, u32[]{:S(2)}, u32[]{:S(2)}) %collective-permute-start.22) | collective-permute-done | bytes 196640 | tf_op jit(solution)/shard_map/ppermute | solution.py:291
  179.5 0.1 add_convert_fusion.2
  179.5 0.1 collective-permute-start.23
  180.3 4.5 %queue.1 = bf16[768,1024]{1,0:T(8,128)(2,1)} custom-call(s32[1]{0:T(128)S(6)} %select_n.63.shift, bf16[768,1024]{1,0:T(8,128)(2,1)} %keys.1, bf16[768,1024]{1,0:T(8,128)(2,1)} %fresh.1), custom_call_target="tpu_custom_call" | custom-call | flops 1207959552 | bytes 5000000 | tf_op jit(solution)/shard_map/queue/pallas_call | solution.py:312
  184.8 0.6 reduce.9
  185.4 1.1 collective-permute-done.23.first
  186.5 0.7 copy-done.2
  187.2 3.5 %final.1 = bf16[96,1024]{1,0:T(8,128)(2,1)} custom-call(bf16[96,1024]{1,0:T(8,128)(2,1)} %copy-done.2, bf16[96,1024]{1,0:T(8,128)(2,1)} %copy-done.1, bf16[96,1024]{1,0:T(8,128)(2,1)} %get-tuple-element.32.own, f32[96,1024]{1,0:T(8,128)} %get-tuple-element.33.hidden, f32[1,1024]{1,0:T(1,128)} %bitcast.12, bf16[1024,1024]{1,0:T(8,128)(2,1)} %get-tuple-element.34.weight), custom_call_target="tpu_custom_call" | custom-call | flops 201326592 | bytes 3500000 | tf_op jit(solution)/shard_map/final/pallas_call | solution.py:298
  (35 shorter events, 0.2 us)
Async XLA Ops:
  0.6 37.9 %collective-permute-start.15 = (bf16[768,1024]{1,0:T(8,128)(2,1)}, bf16[768,1024]{1,0:T(8,128)(2,1)S(1)}, u32[]{:S(2)}, u32[]{:S(2)}) collective-permute-start(bf16[768,1024]{1,0:T(8,128)(2,1)} %keys.1), channel_id=1, source_target_pairs={{0,128},{8,136},{16,144},{24,152},{32,160},{40,168},{48,176},{56,1... | collective-permute-start | bytes 4718600 | tf_op jit(solution)/shard_map/ppermute | solution.py:200
  3.0 90.0 %collective-permute-start.14 = (bf16[768,1024]{1,0:T(8,128)(2,1)}, bf16[768,1024]{1,0:T(8,128)(2,1)S(1)}, u32[]{:S(2)}, u32[]{:S(2)}) collective-permute-start(bf16[768,1024]{1,0:T(8,128)(2,1)} %keys.1), channel_id=1, source_target_pairs={{0,8},{8,0},{16,24},{24,16},{32,40},{40,32},{48,56},{56,48},{64,72... | collective-permute-start | bytes 4718600 | tf_op jit(solution)/shard_map/ppermute | solution.py:201
  38.6 54.4 %copy-start.6 = (bf16[768,1024]{1,0:T(8,128)(2,1)}, bf16[768,1024]{1,0:T(8,128)(2,1)S(1)}, u32[]{:S(2)}) copy-start(bf16[768,1024]{1,0:T(8,128)(2,1)S(1)} %collective-permute-done.15.refs_19_.refs_2_) | copy-start | bytes 4718596
  38.6 54.4 %collective-permute-start.16 = (bf16[768,1024]{1,0:T(8,128)(2,1)S(1)}, bf16[768,1024]{1,0:T(8,128)(2,1)}, u32[]{:S(2)}, u32[]{:S(2)}) collective-permute-start(bf16[768,1024]{1,0:T(8,128)(2,1)S(1)} %collective-permute-done.15.refs_19_.refs_2_), channel_id=1, source_target_pairs={{0,8},{8,0},{16,24},{24,16},{32,40},{40,32},{48,56},{56,48},{64,72... | collective-permute-start | bytes 4718600 | tf_op jit(solution)/shard_map/ppermute | solution.py:202
  40.3 52.7 %copy-start = (bf16[96,1152]{1,0:T(8,128)(2,1)}, bf16[96,1152]{1,0:T(8,128)(2,1)S(1)}, u32[]{:S(2)}) copy-start(bf16[96,1152]{1,0:T(8,128)(2,1)S(1)} %fusion.1.refs_0_) | copy-start | bytes 663556
  40.3 12.0 %collective-permute-start = (bf16[96,1152]{1,0:T(8,128)(2,1)S(1)}, bf16[96,1152]{1,0:T(8,128)(2,1)S(1)}, u32[]{:S(2)}, u32[]{:S(2)}) collective-permute-start(bf16[96,1152]{1,0:T(8,128)(2,1)S(1)} %fusion.1.refs_0_), channel_id=1, source_target_pairs={{0,16},{8,24},{16,32},{24,40},{32,48},{40,56},{48,64},{56,72},{64,... | collective-permute-start | bytes 663560 | tf_op jit(solution)/shard_map/ppermute | solution.py:212
  42.3 13.2 %collective-permute-start.1 = (bf16[96,1152]{1,0:T(8,128)(2,1)S(1)}, bf16[96,1152]{1,0:T(8,128)(2,1)S(1)}, u32[]{:S(2)}, u32[]{:S(2)}) collective-permute-start(bf16[96,1152]{1,0:T(8,128)(2,1)S(1)} %fusion.1.refs_0_), channel_id=1, source_target_pairs={{0,112},{8,120},{16,0},{24,8},{32,16},{40,24},{48,32},{56,40},{64,... | collective-permute-start | bytes 663560 | tf_op jit(solution)/shard_map/ppermute | solution.py:214
  46.4 10.3 %collective-permute-start.7 = (bf16[1024,128]{1,0:T(8,128)(2,1)}, bf16[1024,128]{1,0:T(8,128)(2,1)}, u32[]{:S(2)}, u32[]{:S(2)}) collective-permute-start(bf16[1024,128]{1,0:T(8,128)(2,1)} %refs_8_.1), channel_id=1, source_target_pairs={{0,1},{1,0},{2,3},{3,2},{4,5},{5,4},{6,7},{7,6},{8,9},{9,8},{10,11... | collective-permute-start | bytes 786440 | tf_op jit(solution)/shard_map/ppermute | solution.py:216
  52.4 16.4 %copy-start.8 = (bf16[96,1152]{1,0:T(8,128)(2,1)}, bf16[96,1152]{1,0:T(8,128)(2,1)S(1)}, u32[]{:S(2)}) copy-start(bf16[96,1152]{1,0:T(8,128)(2,1)S(1)} %collective-permute-done.refs_1_) | copy-start | bytes 663556
  52.4 10.9 %collective-permute-start.8 = (bf16[1024,128]{1,0:T(8,128)(2,1)}, bf16[1024,128]{1,0:T(8,128)(2,1)}, u32[]{:S(2)}, u32[]{:S(2)}) collective-permute-start(bf16[1024,128]{1,0:T(8,128)(2,1)} %refs_8_.1), channel_id=1, source_target_pairs={{0,2},{1,3},{2,0},{3,1},{4,6},{5,7},{6,4},{7,5},{8,10},{9,11},{10,... | collective-permute-start | bytes 786440 | tf_op jit(solution)/shard_map/ppermute | solution.py:216
  55.6 21.8 %copy-start.9 = (bf16[96,1152]{1,0:T(8,128)(2,1)}, bf16[96,1152]{1,0:T(8,128)(2,1)S(1)}, u32[]{:S(2)}) copy-start(bf16[96,1152]{1,0:T(8,128)(2,1)S(1)} %collective-permute-done.1.refs_2_) | copy-start | bytes 663556
  55.6 13.2 %collective-permute-start.9 = (bf16[1024,128]{1,0:T(8,128)(2,1)}, bf16[1024,128]{1,0:T(8,128)(2,1)}, u32[]{:S(2)}, u32[]{:S(2)}) collective-permute-start(bf16[1024,128]{1,0:T(8,128)(2,1)} %refs_8_.1), channel_id=1, source_target_pairs={{0,3},{1,2},{2,1},{3,0},{4,7},{5,6},{6,5},{7,4},{8,11},{9,10},{10,... | collective-permute-start | bytes 786440 | tf_op jit(solution)/shard_map/ppermute | solution.py:216
  56.6 12.2 %collective-permute-start.10 = (bf16[1024,128]{1,0:T(8,128)(2,1)}, bf16[1024,128]{1,0:T(8,128)(2,1)}, u32[]{:S(2)}, u32[]{:S(2)}) collective-permute-start(bf16[1024,128]{1,0:T(8,128)(2,1)} %refs_8_.1), channel_id=1, source_target_pairs={{0,4},{1,5},{2,6},{3,7},{4,0},{5,1},{6,2},{7,3},{8,12},{9,13},{10,... | collective-permute-start | bytes 786440 | tf_op jit(solution)/shard_map/ppermute | solution.py:216
  63.3 8.8 %collective-permute-start.11 = (bf16[1024,128]{1,0:T(8,128)(2,1)}, bf16[1024,128]{1,0:T(8,128)(2,1)}, u32[]{:S(2)}, u32[]{:S(2)}) collective-permute-start(bf16[1024,128]{1,0:T(8,128)(2,1)} %refs_8_.1), channel_id=1, source_target_pairs={{0,5},{1,4},{2,7},{3,6},{4,1},{5,0},{6,3},{7,2},{8,13},{9,12},{10,... | collective-permute-start | bytes 786440 | tf_op jit(solution)/shard_map/ppermute | solution.py:216
  68.8 8.6 %collective-permute-start.2 = (bf16[96,1152]{1,0:T(8,128)(2,1)S(1)}, bf16[96,1152]{1,0:T(8,128)(2,1)S(1)}, u32[]{:S(2)}, u32[]{:S(2)}) collective-permute-start(bf16[96,1152]{1,0:T(8,128)(2,1)S(1)} %collective-permute-done.refs_1_), channel_id=1, source_target_pairs={{0,16},{8,24},{16,32},{24,40},{32,48},{40,56},{48,64},{56,72},{64,... | collective-permute-start | bytes 663560 | tf_op jit(solution)/shard_map/ppermute | solution.py:212
  68.8 11.0 %collective-permute-start.12 = (bf16[1024,128]{1,0:T(8,128)(2,1)}, bf16[1024,128]{1,0:T(8,128)(2,1)}, u32[]{:S(2)}, u32[]{:S(2)}) collective-permute-start(bf16[1024,128]{1,0:T(8,128)(2,1)} %refs_8_.1), channel_id=1, source_target_pairs={{0,6},{1,7},{2,4},{3,5},{4,2},{5,3},{6,0},{7,1},{8,14},{9,15},{10,... | collective-permute-start | bytes 786440 | tf_op jit(solution)/shard_map/ppermute | solution.py:216
  72.1 10.6 %collective-permute-start.3 = (bf16[96,1152]{1,0:T(8,128)(2,1)S(1)}, bf16[96,1152]{1,0:T(8,128)(2,1)}, u32[]{:S(2)}, u32[]{:S(2)}) collective-permute-start(bf16[96,1152]{1,0:T(8,128)(2,1)S(1)} %collective-permute-done.1.refs_2_), channel_id=1, source_target_pairs={{0,112},{8,120},{16,0},{24,8},{32,16},{40,24},{48,32},{56,40},{64,... | collective-permute-start | bytes 663560 | tf_op jit(solution)/shard_map/ppermute | solution.py:214
  77.4 5.3 %copy-start.10 = (bf16[96,1152]{1,0:T(8,128)(2,1)}, bf16[96,1152]{1,0:T(8,128)(2,1)S(1)}, u32[]{:S(2)}) copy-start(bf16[96,1152]{1,0:T(8,128)(2,1)S(1)} %collective-permute-done.2.refs_3_) | copy-start | bytes 663556
  77.4 8.2 %collective-permute-start.4 = (bf16[96,1152]{1,0:T(8,128)(2,1)S(1)}, bf16[96,1152]{1,0:T(8,128)(2,1)}, u32[]{:S(2)}, u32[]{:S(2)}) collective-permute-start(bf16[96,1152]{1,0:T(8,128)(2,1)S(1)} %collective-permute-done.2.refs_3_), channel_id=1, source_target_pairs={{0,16},{8,24},{16,32},{24,40},{32,48},{40,56},{48,64},{56,72},{64,... | collective-permute-start | bytes 663560 | tf_op jit(solution)/shard_map/ppermute | solution.py:212
  79.8 9.8 %collective-permute-start.13 = (bf16[1024,128]{1,0:T(8,128)(2,1)}, bf16[1024,128]{1,0:T(8,128)(2,1)}, u32[]{:S(2)}, u32[]{:S(2)}) collective-permute-start(bf16[1024,128]{1,0:T(8,128)(2,1)} %refs_8_.1), channel_id=1, source_target_pairs={{0,7},{1,6},{2,5},{3,4},{4,3},{5,2},{6,1},{7,0},{8,15},{9,14},{10,... | collective-permute-start | bytes 786440 | tf_op jit(solution)/shard_map/ppermute | solution.py:216
  82.7 7.0 %collective-permute-start.5 = (bf16[96,1152]{1,0:T(8,128)(2,1)}, bf16[96,1152]{1,0:T(8,128)(2,1)}, u32[]{:S(2)}, u32[]{:S(2)}) collective-permute-start(bf16[96,1152]{1,0:T(8,128)(2,1)} %collective-permute-done.3.refs_4_), channel_id=1, source_target_pairs={{0,112},{8,120},{16,0},{24,8},{32,16},{40,24},{48,32},{56,40},{64,... | collective-permute-start | bytes 663560 | tf_op jit(solution)/shard_map/ppermute | solution.py:214
  85.5 7.5 %collective-permute-start.6 = (bf16[96,1152]{1,0:T(8,128)(2,1)}, bf16[96,1152]{1,0:T(8,128)(2,1)}, u32[]{:S(2)}, u32[]{:S(2)}) collective-permute-start(bf16[96,1152]{1,0:T(8,128)(2,1)} %collective-permute-done.4.refs_5_), channel_id=1, source_target_pairs={{0,16},{8,24},{16,32},{24,40},{32,48},{40,56},{48,64},{56,72},{64,... | collective-permute-start | bytes 663560 | tf_op jit(solution)/shard_map/ppermute | solution.py:212
  93.0 1.1 copy-start.7
  119.7 4.1 %collective-permute-start.17 = (f32[8,768]{1,0:T(8,128)}, f32[8,768]{1,0:T(8,128)S(1)}, u32[]{:S(2)}, u32[]{:S(2)}) collective-permute-start(f32[8,768]{1,0:T(8,128)} %get-tuple-element.23.local), channel_id=1, source_target_pairs={{0,16},{8,24},{16,0},{24,8},{32,48},{40,56},{48,32},{56,40},{64,80... | collective-permute-start | bytes 73736 | tf_op jit(solution)/shard_map/ppermute | solution.py:250
  124.8 5.0 %collective-permute-start.18 = (f32[8,768]{1,0:T(8,128)S(1)}, f32[8,768]{1,0:T(8,128)S(1)}, u32[]{:S(2)}, u32[]{:S(2)}) collective-permute-start(f32[8,768]{1,0:T(8,128)S(1)} %select_select_fusion.2), channel_id=1, source_target_pairs={{0,32},{8,40},{16,48},{24,56},{32,0},{40,8},{48,16},{56,24},{64,96... | collective-permute-start | bytes 73736 | tf_op jit(solution)/shard_map/ppermute | solution.py:250
  129.9 18.7 %collective-permute-start.19 = (f32[8,768]{1,0:T(8,128)S(1)}, f32[8,768]{1,0:T(8,128)S(1)}, u32[]{:S(2)}, u32[]{:S(2)}) collective-permute-start(f32[8,768]{1,0:T(8,128)S(1)} %select_select_fusion.1), channel_id=1, source_target_pairs={{0,64},{8,72},{16,80},{24,88},{32,96},{40,104},{48,112},{56,120},{... | collective-permute-start | bytes 73736 | tf_op jit(solution)/shard_map/ppermute | solution.py:250
  153.4 19.3 %copy-start.4 = (bf16[96,1024]{1,0:T(8,128)(2,1)S(1)}, bf16[96,1024]{1,0:T(8,128)(2,1)}, u32[]{:S(2)}) copy-start(bf16[96,1024]{1,0:T(8,128)(2,1)} %get-tuple-element.31) | copy-start | bytes 589828
  153.4 26.1 %copy-start.3 = (bf16[96,1024]{1,0:T(8,128)(2,1)S(1)}, bf16[96,1024]{1,0:T(8,128)(2,1)}, u32[]{:S(2)}) copy-start(bf16[96,1024]{1,0:T(8,128)(2,1)} %get-tuple-element.28) | copy-start | bytes 589828
  153.4 9.0 %collective-permute-start.20 = (bf16[96,1024]{1,0:T(8,128)(2,1)}, bf16[96,1024]{1,0:T(8,128)(2,1)S(1)}, u32[]{:S(2)}, u32[]{:S(2)}) collective-permute-start(bf16[96,1024]{1,0:T(8,128)(2,1)} %get-tuple-element.25), channel_id=1, source_target_pairs={{0,16},{8,24},{16,32},{24,40},{32,48},{40,56},{48,64},{56,72},{64,... | collective-permute-start | bytes 589832 | tf_op jit(solution)/shard_map/ppermute | solution.py:291
  153.6 9.9 %collective-permute-start.24 = (bf16[96,1024]{1,0:T(8,128)(2,1)}, bf16[96,1024]{1,0:T(8,128)(2,1)S(1)}, u32[]{:S(2)}, u32[]{:S(2)}) collective-permute-start(bf16[96,1024]{1,0:T(8,128)(2,1)} %get-tuple-element.29), channel_id=1, source_target_pairs={{0,112},{8,120},{16,0},{24,8},{32,16},{40,24},{48,32},{56,40},{64,... | collective-permute-start | bytes 589832 | tf_op jit(solution)/shard_map/ppermute | solution.py:294
  163.3 8.2 %collective-permute-start.21 = (bf16[96,1024]{1,0:T(8,128)(2,1)S(1)}, bf16[96,1024]{1,0:T(8,128)(2,1)S(1)}, u32[]{:S(2)}, u32[]{:S(2)}) collective-permute-start(bf16[96,1024]{1,0:T(8,128)(2,1)S(1)} %add_convert_fusion.4), channel_id=1, source_target_pairs={{0,16},{8,24},{16,32},{24,40},{32,48},{40,56},{48,64},{56,72},{64,... | collective-permute-start | bytes 589832 | tf_op jit(solution)/shard_map/ppermute | solution.py:291
  164.4 8.2 %collective-permute-start.25 = (bf16[96,1024]{1,0:T(8,128)(2,1)S(1)}, bf16[96,1024]{1,0:T(8,128)(2,1)S(1)}, u32[]{:S(2)}, u32[]{:S(2)}) collective-permute-start(bf16[96,1024]{1,0:T(8,128)(2,1)S(1)} %add_convert_fusion.1), channel_id=1, source_target_pairs={{0,112},{8,120},{16,0},{24,8},{32,16},{40,24},{48,32},{56,40},{64,... | collective-permute-start | bytes 589832 | tf_op jit(solution)/shard_map/ppermute | solution.py:294
  172.5 7.0 %collective-permute-start.22 = (bf16[96,1024]{1,0:T(8,128)(2,1)S(1)}, bf16[96,1024]{1,0:T(8,128)(2,1)S(1)}, u32[]{:S(2)}, u32[]{:S(2)}) collective-permute-start(bf16[96,1024]{1,0:T(8,128)(2,1)S(1)} %add_convert_fusion.3), channel_id=1, source_target_pairs={{0,16},{8,24},{16,32},{24,40},{32,48},{40,56},{48,64},{56,72},{64,... | collective-permute-start | bytes 589832 | tf_op jit(solution)/shard_map/ppermute | solution.py:291
  172.7 12.7 %collective-permute-start.26 = (bf16[96,1024]{1,0:T(8,128)(2,1)S(1)}, bf16[96,1024]{1,0:T(8,128)(2,1)S(1)}, u32[]{:S(2)}, u32[]{:S(2)}) collective-permute-start(bf16[96,1024]{1,0:T(8,128)(2,1)S(1)} %add_convert_fusion), channel_id=1, source_target_pairs={{0,112},{8,120},{16,0},{24,8},{32,16},{40,24},{48,32},{56,40},{64,... | collective-permute-start | bytes 589832 | tf_op jit(solution)/shard_map/ppermute | solution.py:294
  179.5 7.0 %collective-permute-start.23 = (bf16[96,1024]{1,0:T(8,128)(2,1)S(1)}, bf16[96,1024]{1,0:T(8,128)(2,1)S(1)}, u32[]{:S(2)}, u32[]{:S(2)}) collective-permute-start(bf16[96,1024]{1,0:T(8,128)(2,1)S(1)} %add_convert_fusion.2), channel_id=1, source_target_pairs={{0,16},{8,24},{16,32},{24,40},{32,48},{40,56},{48,64},{56,72},{64,... | collective-permute-start | bytes 589832 | tf_op jit(solution)/shard_map/ppermute | solution.py:291
  180.3 4.5 %copy-start.5 = (f32[96,1]{1,0:T(8,128)S(1)}, f32[96,1]{1,0:T(8,128)}, u32[]{:S(2)}) copy-start(f32[96,1]{1,0:T(8,128)} %get-tuple-element.24) | copy-start | bytes 1156
  185.4 1.1 copy-start.1
  186.5 0.7 copy-start.2

commit v2 on v1

v2 whole, which is shorter than its diff:
```python
import functools
import math

import jax
import jax.numpy as jnp
from jax import lax
from jax.experimental import pallas as pl
from jax.experimental.pallas import tpu as pltpu
from jax.sharding import PartitionSpec as P

RING = 8
BIG = 56 * 1024 * 1024
F32 = jnp.float32
BF16 = jnp.bfloat16
GATHER = (0, -1, 1, -2, 2, -3, 3, -4)
REDUCE = (4, -3, 3, -2, 2, -1, 1, 0)


def vmem():
    return pl.BlockSpec(memory_space=pltpu.VMEM)


def smem():
    return pl.BlockSpec(memory_space=pltpu.SMEM)


def queue_perm(move):
    def index(x, z, c):
        return (x * RING + z) * 2 + c

    return [
        (index(x, z, c), index(*move(x, z, c)))
        for x in range(2)
        for z in range(RING)
        for c in range(2)
    ]


UP = queue_perm(lambda x, z, c: (x, (z + 1) % RING, c))
DOWN = queue_perm(lambda x, z, c: (x, (z - 1) % RING, c))
CORE = queue_perm(lambda x, z, c: (x, z, 1 - c))
FAR = queue_perm(lambda x, z, c: (1 - x, z, c))


def picked_kernel(rows, place, *refs):
    slots, keys, out, chosen = refs[:RING], refs[RING : RING + 4], refs[RING + 4], refs[RING + 5]
    z = place[0]
    width, count = out.shape[1], keys[0].shape[0]
    for slot, offset in enumerate(GATHER):
        start = pl.multiple_of(lax.rem(z + offset + RING, RING) * rows, rows)
        codes = slots[slot][:, width:].astype(F32)
        ids = (codes[:, 0:1] * 128.0 + codes[:, 1:2]).astype(jnp.int32)
        for j in range(4):
            mine = lax.broadcasted_iota(jnp.int32, (rows, count), 1) == ids - place[3 + j]
            chosen[pl.ds(start, rows), j * count : (j + 1) * count] = mine.astype(F32).astype(BF16)
    tile = 256

    @pl.loop(0, width // tile)
    def _(t):
        columns = pl.ds(pl.multiple_of(t * tile, tile), tile)
        total = jnp.zeros((out.shape[0], tile), F32)
        for j in range(4):
            total += jnp.dot(
                chosen[:, j * count : (j + 1) * count],
                keys[j][:, columns],
                preferred_element_type=F32,
            )
        out[:, columns] = total.astype(BF16)


def score_kernel(factor, rows, place, *refs):
    slots = refs[:RING]
    mine_weight, other_weight, gain = refs[RING : RING + 3]
    keys = refs[RING + 3 : RING + 7]
    outs = refs[RING + 7 : 2 * RING + 7]
    own_hidden, full_weight = refs[2 * RING + 7 : 2 * RING + 9]
    speech, hidden, queries, scores, probs, wanted, peaks, table = refs[2 * RING + 9 :]
    z, core = place[0], place[2]
    width = hidden.shape[1]
    count = keys[0].shape[0]
    piece = mine_weight.shape[1]
    half = mine_weight.shape[0] // 8

    for m in range(8):
        columns = slice(m * piece, (m + 1) * piece)
        block = slice(m * half, (m + 1) * half)
        full_weight[pl.ds(pl.multiple_of(core * half, half), half), columns] = mine_weight[block, :]
        full_weight[pl.ds(pl.multiple_of((1 - core) * half, half), half), columns] = other_weight[
            block, :
        ]
    for slot, offset in enumerate(GATHER):
        owner = lax.rem(z + offset + RING, RING)
        start = pl.multiple_of(owner * rows, rows)
        speech[pl.ds(start, rows), :] = slots[slot][:, :width]
        codes = slots[slot][:, width:].astype(F32)
        ids = codes[:, 0:1] * 128.0 + codes[:, 1:2]
        wanted[pl.ds(start, rows), :] = jnp.broadcast_to(ids, (rows, 128))

    tile = 256

    @pl.loop(0, width // tile)
    def _(t):
        columns = pl.ds(pl.multiple_of(t * tile, tile), tile)
        hidden[:, columns] = jnp.dot(
            speech[...], full_weight[:, columns], preferred_element_type=F32
        )

    @pl.loop(0, RING)
    def _(b):
        span = pl.ds(pl.multiple_of(b * rows, rows), rows)
        block = hidden[span, :]
        inverse = lax.rsqrt(jnp.mean(block * block, axis=1, keepdims=True) + 1e-06)
        queries[span, :] = (block * inverse * gain[...]).astype(BF16)

    own_hidden[...] = hidden[pl.ds(pl.multiple_of(z * rows, rows), rows), :]
    peaks[...] = jnp.full(peaks.shape, -3e38, F32)

    for j in range(4):

        @pl.loop(0, count // tile)
        def _(t, j=j):
            key_rows = keys[j][pl.ds(pl.multiple_of(t * tile, tile), tile), :]
            product = (
                lax.dot_general(
                    queries[...], key_rows, (((1,), (1,)), ((), ())), preferred_element_type=F32
                )
                * factor
            )
            start = pl.multiple_of(j * count + t * tile, tile)
            scores[:, pl.ds(start, tile)] = product
            peaks[...] = jnp.maximum(
                peaks[...], jnp.maximum(product[:, :128], product[:, 128:])
            )

    step_rows = 32

    @pl.loop(0, RING * rows // step_rows)
    def _(b):
        span = pl.ds(pl.multiple_of(b * step_rows, step_rows), step_rows)
        peak = jnp.max(peaks[span, :], axis=1, keepdims=True).astype(BF16).astype(F32)
        ids = wanted[span, 0:1].astype(jnp.int32)
        partial = jnp.zeros((step_rows, 128), F32)
        for j in range(4):
            mine = lax.broadcasted_iota(jnp.int32, (step_rows, count), 1) == ids - place[3 + j]
            powers = jnp.exp(scores[span, j * count : (j + 1) * count] - peak)
            powers = jnp.where(mine, 0.0, powers)
            probs[span, j * count : (j + 1) * count] = powers.astype(BF16)
            for g in range(count // 128):
                partial += powers[:, g * 128 : (g + 1) * 128]
        total = jnp.sum(partial, axis=1, keepdims=True)
        table[span, :] = tail(peak, total)

    @pl.loop(0, width // tile)
    def _(t):
        columns = pl.ds(pl.multiple_of(t * tile, tile), tile)
        total = jnp.zeros((RING * rows, tile), F32)
        for j in range(4):
            total += jnp.dot(
                probs[:, j * count : (j + 1) * count],
                keys[j][:, columns],
                preferred_element_type=F32,
            )
        hidden[:, columns] = total

    for slot, offset in enumerate(REDUCE):
        start = pl.multiple_of(lax.rem(z + offset + RING, RING) * rows, rows)
        outs[slot][:, :width] = hidden[pl.ds(start, rows), :].astype(BF16)
        outs[slot][:, width:] = table[pl.ds(start, rows), :]


def tail(peak, total):
    lane = lax.broadcasted_iota(jnp.int32, (peak.shape[0], 128), 1)
    high = total.astype(BF16).astype(F32)
    columns = jnp.where(lane == 0, peak, jnp.where(lane == 1, high, total - high))
    return jnp.where(lane < 3, columns, 0.0).astype(BF16)


def split(block, width):
    end = block[:, width:].astype(F32)
    return (block[:, :width].astype(F32), end[:, 0:1], end[:, 1:2] + end[:, 2:3])


def join(first, second):
    peak = jnp.maximum(first[1], second[1])
    left, right = jnp.exp(first[1] - peak), jnp.exp(second[1] - peak)
    return (first[0] * left + second[0] * right, peak, first[2] * left + second[2] * right)


def merge_kernel(width, first, second, out):
    sums, peak, total = join(split(first[...], width), split(second[...], width))
    out[:, :width] = sums.astype(BF16)
    out[:, width:] = tail(peak, total)


def final_kernel(factor, first, second, own, hidden, gain, picked, weight, out, loss):
    width = hidden.shape[1]
    merged = join(split(first[...], width), split(second[...], width))
    sums, peak, total = join(merged, split(own[...], width))
    values = hidden[...]
    inverse = lax.rsqrt(jnp.mean(values * values, axis=1, keepdims=True) + 1e-06)
    queries = (values * inverse * gain[...]).astype(BF16).astype(F32)
    positive = picked[...].astype(F32)
    score = jnp.sum(queries * positive, axis=1, keepdims=True) * factor
    top = jnp.maximum(peak, score)
    others = jnp.exp(peak - top)
    whole = total * others + jnp.exp(score - top)
    loss[...] = top + jnp.log(whole) - score
    share = others / whole
    grad = (sums * share - positive * (total * share)) * (16.0 * factor)
    scaled = gain[...] * grad
    inner = jnp.sum(scaled * values, axis=1, keepdims=True)
    hidden_grad = (
        inverse * scaled - values * (inverse * inverse * inverse) * inner / width
    ).astype(BF16)
    out[...] = lax.dot_general(
        hidden_grad, weight[...], (((1,), (1,)), ((), ())), preferred_element_type=F32
    ).astype(BF16)


def queue_kernel(shift, keys, fresh, out):
    count = keys.shape[0]
    wanted = lax.broadcasted_iota(jnp.int32, (count, 1), 0) + shift[0]
    pick = lax.broadcasted_iota(jnp.int32, (count, fresh.shape[0]), 1) == wanted
    moved = jnp.dot(pick.astype(F32).astype(BF16), fresh[...], preferred_element_type=F32)
    replaced = (wanted >= 0) & (wanted < fresh.shape[0])
    out[...] = jnp.where(replaced, moved, keys[...].astype(F32)).astype(BF16)


def shards(speech, weight, norm_gain, queue_keys, new_keys, pointer, positives):
    rows, width = speech.shape
    count = queue_keys.shape[0]
    total_rows = RING * rows
    queue_length = count * lax.axis_size("queue")
    queue_index = lax.axis_index("queue")
    mp = lax.axis_index("mp")
    z = (queue_index // 2) % RING
    factor = 2.0 / math.sqrt(width)
    params = pltpu.CompilerParams(vmem_limit_bytes=BIG)

    core = queue_index % 2
    far = lax.ppermute(queue_keys, "queue", FAR)
    near = lax.ppermute(queue_keys, "queue", CORE)
    flipped = queue_index ^ (2 * RING)
    bases = [index * count for index in (queue_index, queue_index ^ 1, flipped, flipped ^ 1)]
    place = jnp.stack([z, mp, core] + bases).astype(jnp.int32)

    codes = jnp.stack([positives // 128, positives % 128], axis=1).astype(BF16)
    packed = jnp.concatenate([speech, jnp.pad(codes, ((0, 0), (0, 126)))], axis=1)
    half = width // 2
    part = lax.dynamic_slice_in_dim(weight, core * half, half, 0)
    part, packed = lax.optimization_barrier((part, packed))
    slots = {0: packed}
    for step in range(1, 5):
        slots[-step] = lax.ppermute(slots[1 - step], "queue", UP)
        if step < 4:
            slots[step] = lax.ppermute(slots[step - 1], "queue", DOWN)
            slots[-step], slots[step] = lax.optimization_barrier((slots[-step], slots[step]))
    mine_weight = lax.all_gather(part, "mp", axis=0, tiled=True)
    far, mine_weight, slots[-4] = lax.optimization_barrier((far, mine_weight, slots[-4]))
    far_near = lax.ppermute(far, "queue", CORE)
    other_weight = lax.ppermute(mine_weight, "queue", CORE)
    far_near, other_weight = lax.optimization_barrier((far_near, other_weight))
    keys = (queue_keys, near, far, far_near)

    gain = norm_gain.reshape(1, width)
    gathered = [slots[offset] for offset in GATHER]

    picked = pl.pallas_call(
        functools.partial(picked_kernel, rows),
        out_shape=jax.ShapeDtypeStruct((total_rows, width), BF16),
        in_specs=[smem()] + [vmem()] * (RING + 4),
        out_specs=vmem(),
        scratch_shapes=[pltpu.VMEM((total_rows, 4 * count), BF16)],
        compiler_params=params,
        cost_estimate=pl.CostEstimate(
            flops=2 * total_rows * width * 4 * count, bytes_accessed=10_000_000, transcendentals=0
        ),
        name="picked",
    )(place, *gathered, *keys)
    groups = [
        [(x * RING + k) * 2 + c for k in range(RING)] for x in range(2) for c in range(2)
    ]
    own_picked = lax.psum_scatter(
        picked, "queue", scatter_dimension=0, axis_index_groups=groups, tiled=True
    )

    block = jax.ShapeDtypeStruct((rows, width + 128), BF16)
    *grads, own_hidden, full_weight = pl.pallas_call(
        functools.partial(score_kernel, factor, rows),
        out_shape=[block] * RING
        + [
            jax.ShapeDtypeStruct((rows, width), F32),
            jax.ShapeDtypeStruct((width, width), BF16),
        ],
        in_specs=[smem()] + [vmem()] * (RING + 3 + 4),
        out_specs=[vmem()] * (RING + 2),
        scratch_shapes=[
            pltpu.VMEM((total_rows, width), BF16),
            pltpu.VMEM((total_rows, width), F32),
            pltpu.VMEM((total_rows, width), BF16),
            pltpu.VMEM((total_rows, 4 * count), F32),
            pltpu.VMEM((total_rows, 4 * count), BF16),
            pltpu.VMEM((total_rows, 128), F32),
            pltpu.VMEM((total_rows, 128), F32),
            pltpu.VMEM((total_rows, 128), BF16),
        ],
        compiler_params=params,
        cost_estimate=pl.CostEstimate(
            flops=2 * total_rows * width * (8 * count + width),
            bytes_accessed=16_000_000,
            transcendentals=total_rows * 4 * count,
        ),
        name="scores",
    )(place, *gathered, mine_weight, other_weight, gain, *keys)
    grads = dict(zip(REDUCE, grads))

    def merge(first, second):
        return pl.pallas_call(
            functools.partial(merge_kernel, width),
            out_shape=block,
            in_specs=[vmem()] * 2,
            out_specs=vmem(),
            compiler_params=params,
            cost_estimate=pl.CostEstimate(
                flops=4 * rows * width, bytes_accessed=600_000, transcendentals=2 * rows
            ),
            name="merge",
        )(first, second)

    first, second = grads[4], grads[-3]
    for step in range(4):
        first = lax.ppermute(first, "queue", UP)
        if step < 3:
            first = merge(first, grads[3 - step])
            second = lax.ppermute(second, "queue", DOWN)
            if step < 2:
                second = merge(second, grads[step - 2])

    grad_speech, losses = pl.pallas_call(
        functools.partial(final_kernel, factor),
        out_shape=(
            jax.ShapeDtypeStruct((rows, width), BF16),
            jax.ShapeDtypeStruct((rows, 1), F32),
        ),
        in_specs=[vmem()] * 7,
        out_specs=(vmem(),) * 2,
        compiler_params=params,
        cost_estimate=pl.CostEstimate(
            flops=2 * rows * width * width, bytes_accessed=3_500_000, transcendentals=rows
        ),
        name="final",
    )(first, second, grads[0], own_hidden, gain, own_picked, full_weight)

    shift = (queue_index * count - pointer) % queue_length
    shift = jnp.where(shift >= queue_length - count, shift - queue_length, shift)
    queue_next = pl.pallas_call(
        queue_kernel,
        out_shape=jax.ShapeDtypeStruct(queue_keys.shape, BF16),
        in_specs=[smem(), vmem(), vmem()],
        out_specs=vmem(),
        compiler_params=params,
        cost_estimate=pl.CostEstimate(
            flops=2 * count * count * width, bytes_accessed=5_000_000, transcendentals=0
        ),
        name="queue",
    )(shift, queue_keys, new_keys)
    return (losses.reshape(rows), grad_speech, queue_next)


def solution(mesh):
    return jax.shard_map(
        shards,
        mesh=mesh,
        in_specs=(
            P(("queue", "mp"), None),
            P(None, "mp"),
            P(),
            P("queue", None),
            P(),
            P(),
            P(("queue", "mp")),
        ),
        out_specs=(P(("queue", "mp")), P(("queue", "mp"), None), P("queue", None)),
        check_vma=False,
    )
```

time: 191 us -> 167 us (0.87)
  waiting for transfers between devices: 85.7 us -> 52.5 us
  between operations: 1.51 us -> 14.9 us
  starting transfers between devices: 41.4 us -> 28.6 us
  Pallas kernels: 52.3 us -> 60.7 us
  other arithmetic: 7.11 us -> 3.08 us
  local copies, waits for them, and re-layouts: 2.65 us -> 6.33 us
    ppermute x1, waiting for transfers between devices: 35.6 us -> 12.8 us  [shards(): far = lax.ppermute(queue_keys, 'queue', FAR)]
    ppermute x10 -> x1, waiting for transfers between devices: 25.4 us -> 5.79 us  [shards(): other_weight = lax.ppermute(mine_weight, 'queue', CORE)]
    ppermute x10 -> x1, starting transfers between devices: 17.6 us -> 0.28 us  [shards(): other_weight = lax.ppermute(mine_weight, 'queue', CORE)]
    pallas_call x4 -> x8, Pallas kernels: 47.8 us -> 56.2 us  [the longest x1 30.2 us: shards(): pl.pallas_call(functools.partial(score_kernel, factor, rows), out_shape=[...]
    ppermute x4, waiting for transfers between devices: 10.8 us -> 18.4 us  [shards(): slots[-step] = lax.ppermute(slots[1 - step], 'queue', UP)]
    convert_element_type x5 -> x0, other arithmetic: 3.04 us -> none  [the longest x3 2.01 us: shards(): first = (first.astype(F32) + grads[3 - step].astype(F32)).astype(BF16)]
    unnamed x22 -> x36, local copies, waits for them, and re-layouts: 1.84 us -> 4.86 us
    ppermute x4, starting transfers between devices: 2 us -> 4.3 us  [shards(): slots[-step] = lax.ppermute(slots[1 - step], 'queue', UP)]
  transfers between devices with their start and end apart: 27 -> 20, of which waited for: 15 -> 11; matrix products, arithmetic and copies ran while one was open for 3% -> 0% of each run, Pallas kernels for 10% -> 27%
where the time goes in v2:
time: 167 us; the launch traced here: 166 us
  Pallas kernels  60.7 us (36%)
  waiting for transfers between devices  52.5 us (31%)
  starting transfers between devices  28.6 us (17%)
  between operations  14.9 us (9%)
  local copies, waits for them, and re-layouts  6.33 us (4%)
  other arithmetic  3.08 us (2%)
    pallas_call x1, Pallas kernels, shards(): pl.pallas_call(functools.partial(score_kernel, factor, rows), out_shape=[...  30.2 us
    ppermute x4, waiting for transfers between devices, shards(): slots[-step] = lax.ppermute(slots[1 - step], 'queue', UP)  18.4 us
    ppermute x4, waiting for transfers between devices, shards(): first = lax.ppermute(first, 'queue', UP)  14.7 us
    ppermute x1, waiting for transfers between devices, shards(): far = lax.ppermute(queue_keys, 'queue', FAR)  12.8 us
    pallas_call x1, Pallas kernels, shards(): pl.pallas_call(functools.partial(picked_kernel, rows), out_shape=jax.Shap...  11.9 us
    ppermute x3, starting transfers between devices, shards(): second = lax.ppermute(second, 'queue', DOWN)  10.5 us
    pallas_call x5, Pallas kernels, merge(): pl.pallas_call(functools.partial(merge_kernel, width), out_shape=block, i...  9.93 us
    ppermute x3, starting transfers between devices, shards(): slots[step] = lax.ppermute(slots[step - 1], 'queue', DOWN)  8.45 us
  transfers between devices with their start and end apart: 20, of which 11 were waited for; matrix products, arithmetic and copies ran while one was open for 0% of the time, Pallas kernels for 27%

profile of v2, /device:TPU:4, one launch (start us, length us, event | category | flops | bytes accessed | tf_op | source)
XLA Modules:
  0.0 166.1 jit_solution(17177008131571573696)
XLA Ops:
  7.2 0.0 copy-start
  7.2 0.0 all-gather.2.cloned.1.call-start
  7.2 0.7 convert_bitcast_fusion
  8.0 0.1 copy.14
  8.1 0.0 copy-done
  8.1 0.7 constant_dynamic-slice_fusion
  8.8 0.9 fusion.1.refs_0_
  9.7 0.0 all-gather.2.cloned.1.call-update
  9.8 0.0 reduce-scatter.2.cloned.1.call-start
  9.8 2.3 %collective-permute-start.6 = (bf16[768,1024]{1,0:T(8,128)(2,1)}, bf16[768,1024]{1,0:T(8,128)(2,1)S(1)}, u32[]{:S(2)}, u32[]{:S(2)}) collective-permute-start(bf16[768,1024]{1,0:T(8,128)(2,1)} %keys.1), channel_id=1, source_target_pairs={{0,128},{8,136},{16,144},{24,152},{32,160},{40,168},{48,176},{56,1... | collective-permute-start | bytes 4718600 | tf_op jit(solution)/shard_map/ppermute | solution.py:241
  12.1 0.2 collective-permute-start
  12.3 3.9 %collective-permute-start.1 = (bf16[96,1152]{1,0:T(8,128)(2,1)S(1)}, bf16[96,1152]{1,0:T(8,128)(2,1)S(1)}, u32[]{:S(2)}, u32[]{:S(2)}) collective-permute-start(bf16[96,1152]{1,0:T(8,128)(2,1)S(1)} %fusion.1.refs_0_), channel_id=1, source_target_pairs={{0,112},{8,120},{16,0},{24,8},{32,16},{40,24},{48,32},{56,40},{64,... | collective-permute-start | bytes 663560 | tf_op jit(solution)/shard_map/ppermute | solution.py:256
  16.3 5.1 %collective-permute-done.refs_1_ = bf16[96,1152]{1,0:T(8,128)(2,1)S(1)} collective-permute-done((bf16[96,1152]{1,0:T(8,128)(2,1)S(1)}, bf16[96,1152]{1,0:T(8,128)(2,1)S(1)}, u32[]{:S(2)}, u32[]{:S(2)}) %collective-permute-start) | collective-permute-done | bytes 221216 | tf_op jit(solution)/shard_map/ppermute | solution.py:254
  21.4 0.0 collective-permute-done.1.refs_2_
  21.4 0.1 collective-permute-start.2
  21.5 3.2 %collective-permute-start.3 = (bf16[96,1152]{1,0:T(8,128)(2,1)S(1)}, bf16[96,1152]{1,0:T(8,128)(2,1)S(1)}, u32[]{:S(2)}, u32[]{:S(2)}) collective-permute-start(bf16[96,1152]{1,0:T(8,128)(2,1)S(1)} %collective-permute-done.1.refs_2_), channel_id=1, source_target_pairs={{0,112},{8,120},{16,0},{24,8},{32,16},{40,24},{48,32},{56,40},{64,... | collective-permute-start | bytes 663560 | tf_op jit(solution)/shard_map/ppermute | solution.py:256
  24.7 4.3 %collective-permute-done.2.refs_3_ = bf16[96,1152]{1,0:T(8,128)(2,1)S(1)} collective-permute-done((bf16[96,1152]{1,0:T(8,128)(2,1)S(1)}, bf16[96,1152]{1,0:T(8,128)(2,1)S(1)}, u32[]{:S(2)}, u32[]{:S(2)}) %collective-permute-start.2) | collective-permute-done | bytes 221216 | tf_op jit(solution)/shard_map/ppermute | solution.py:254
  29.0 0.0 collective-permute-done.3.refs_4_
  29.0 2.0 %collective-permute-start.4 = (bf16[96,1152]{1,0:T(8,128)(2,1)S(1)}, bf16[96,1152]{1,0:T(8,128)(2,1)S(1)}, u32[]{:S(2)}, u32[]{:S(2)}) collective-permute-start(bf16[96,1152]{1,0:T(8,128)(2,1)S(1)} %collective-permute-done.2.refs_3_), channel_id=1, source_target_pairs={{0,16},{8,24},{16,32},{24,40},{32,48},{40,56},{48,64},{56,72},{64,... | collective-permute-start | bytes 663560 | tf_op jit(solution)/shard_map/ppermute | solution.py:254
  31.0 1.3 collective-permute-start.5
  32.3 3.9 %collective-permute-done.4.refs_5_ = bf16[96,1152]{1,0:T(8,128)(2,1)S(1)} collective-permute-done((bf16[96,1152]{1,0:T(8,128)(2,1)S(1)}, bf16[96,1152]{1,0:T(8,128)(2,1)S(1)}, u32[]{:S(2)}, u32[]{:S(2)}) %collective-permute-start.4) | collective-permute-done | bytes 221216 | tf_op jit(solution)/shard_map/ppermute | solution.py:254
  36.2 0.7 collective-permute-done.5.refs_6_
  37.0 2.0 %collective-permute-start.7 = (bf16[96,1152]{1,0:T(8,128)(2,1)S(1)}, bf16[96,1152]{1,0:T(8,128)(2,1)S(1)}, u32[]{:S(2)}, u32[]{:S(2)}) collective-permute-start(bf16[96,1152]{1,0:T(8,128)(2,1)S(1)} %collective-permute-done.4.refs_5_), channel_id=1, source_target_pairs={{0,16},{8,24},{16,32},{24,40},{32,48},{40,56},{48,64},{56,72},{64,... | collective-permute-start | bytes 663560 | tf_op jit(solution)/shard_map/ppermute | solution.py:254
  39.0 5.1 %collective-permute-done.7.refs_7_ = bf16[96,1152]{1,0:T(8,128)(2,1)S(1)} collective-permute-done((bf16[96,1152]{1,0:T(8,128)(2,1)S(1)}, bf16[96,1152]{1,0:T(8,128)(2,1)S(1)}, u32[]{:S(2)}, u32[]{:S(2)}) %collective-permute-start.7) | collective-permute-done | bytes 221216 | tf_op jit(solution)/shard_map/ppermute | solution.py:254
  44.1 0.7 copy-done.17
  44.8 12.8 %collective-permute-done.6.refs_13_.refs_10_ = bf16[768,1024]{1,0:T(8,128)(2,1)S(1)} collective-permute-done((bf16[768,1024]{1,0:T(8,128)(2,1)}, bf16[768,1024]{1,0:T(8,128)(2,1)S(1)}, u32[]{:S(2)}, u32[]{:S(2)}) %collective-permute-start.6) | collective-permute-done | bytes 1572896 | tf_op jit(solution)/shard_map/ppermute | solution.py:241
  57.6 0.0 collective-permute-start.8
  57.6 0.6 collective-permute-start.10
  58.2 0.3 collective-permute-start.9
  58.5 0.7 stack.43.place
  59.2 5.8 %collective-permute-done.9.refs_9_ = bf16[4096,128]{1,0:T(8,128)(2,1)S(1)} collective-permute-done((bf16[4096,128]{1,0:T(8,128)(2,1)}, bf16[4096,128]{1,0:T(8,128)(2,1)S(1)}, u32[]{:S(2)}, u32[]{:S(2)}) %collective-permute-start.9) | collective-permute-done | bytes 1048608 | tf_op jit(solution)/shard_map/ppermute | solution.py:261
  65.0 0.0 collective-permute-done.8.refs_14_.refs_11_
  65.0 0.0 collective-permute-done.10.refs_12_.refs_9_
  65.0 11.9 %picked.1 = bf16[768,1024]{1,0:T(8,128)(2,1)} custom-call(s32[7]{0:T(128)} %stack.43.place, bf16[96,1152]{1,0:T(8,128)(2,1)} %copy-done.3, bf16[96,1152]{1,0:T(8,128)(2,1)} %copy-done.11, bf16[96,1152]{1,0:T(8,128)(2,1)} %copy-done.12, bf16[96,1152]{1,0:T(8,128)(2,1)} %copy-done.13, bf16[96,1152]{1,0:T(8,128)(2,1)} %copy-done.14, ...), custom_call_target="tpu_custom_call" | custom-call | flops 4831838208 | bytes 10000000 | tf_op jit(solution)/shard_map/picked/pallas_call | solution.py:268
  76.9 0.0 reduce-scatter.2.cloned.1.call-update
  76.9 30.2 %scores.1 = (bf16[96,1152]{1,0:T(8,128)(2,1)}, bf16[96,1152]{1,0:T(8,128)(2,1)}, bf16[96,1152]{1,0:T(8,128)(2,1)}, bf16[96,1152]{1,0:T(8,128)(2,1)}, bf16[96,115...) custom-call(s32[7]{0:T(128)} %stack.43.place, ...), custom_call_target="tpu_custom_call" | custom-call | flops 11274289152 | bytes 16000000 | tf_op jit(solution)/shard_map/scores/pallas_call | solution.py:288
  107.2 2.1 %collective-permute-start.11 = (bf16[96,1152]{1,0:T(8,128)(2,1)}, bf16[96,1152]{1,0:T(8,128)(2,1)S(1)}, u32[]{:S(2)}, u32[]{:S(2)}) collective-permute-start(bf16[96,1152]{1,0:T(8,128)(2,1)} %get-tuple-element.41), channel_id=1, source_target_pairs={{0,16},{8,24},{16,32},{24,40},{32,48},{40,56},{48,64},{56,72},{64,... | collective-permute-start | bytes 663560 | tf_op jit(solution)/shard_map/ppermute | solution.py:332
  109.3 4.0 %collective-permute-start.15 = (bf16[96,1152]{1,0:T(8,128)(2,1)}, bf16[96,1152]{1,0:T(8,128)(2,1)S(1)}, u32[]{:S(2)}, u32[]{:S(2)}) collective-permute-start(bf16[96,1152]{1,0:T(8,128)(2,1)} %get-tuple-element.45), channel_id=1, source_target_pairs={{0,112},{8,120},{16,0},{24,8},{32,16},{40,24},{48,32},{56,40},{64,... | collective-permute-start | bytes 663560 | tf_op jit(solution)/shard_map/ppermute | solution.py:335
  113.3 7.9 %collective-permute-done.11.first = bf16[96,1152]{1,0:T(8,128)(2,1)S(1)} collective-permute-done((bf16[96,1152]{1,0:T(8,128)(2,1)}, bf16[96,1152]{1,0:T(8,128)(2,1)S(1)}, u32[]{:S(2)}, u32[]{:S(2)}) %collective-permute-start.11) | collective-permute-done | bytes 221216 | tf_op jit(solution)/shard_map/ppermute | solution.py:332
  121.2 0.7 copy-done.8
  121.9 2.0 %merge.5 = bf16[96,1152]{1,0:T(8,128)(2,1)} custom-call(bf16[96,1152]{1,0:T(8,128)(2,1)} %copy-done.8, bf16[96,1152]{1,0:T(8,128)(2,1)} %get-tuple-element.42.second), custom_call_target="tpu_custom_call" | custom-call | flops 393216 | bytes 600000 | tf_op jit(solution)/shard_map/merge/pallas_call | solution.py:318
  123.9 0.0 collective-permute-start.12
  123.9 0.0 collective-permute-done.15.first
  123.9 0.7 copy-done.4
  124.6 2.0 %merge.8 = bf16[96,1152]{1,0:T(8,128)(2,1)} custom-call(bf16[96,1152]{1,0:T(8,128)(2,1)} %copy-done.4, bf16[96,1152]{1,0:T(8,128)(2,1)} %get-tuple-element.46.second), custom_call_target="tpu_custom_call" | custom-call | flops 393216 | bytes 600000 | tf_op jit(solution)/shard_map/merge/pallas_call | solution.py:318
  126.6 3.2 %collective-permute-start.16 = (bf16[96,1152]{1,0:T(8,128)(2,1)}, bf16[96,1152]{1,0:T(8,128)(2,1)S(1)}, u32[]{:S(2)}, u32[]{:S(2)}) collective-permute-start(bf16[96,1152]{1,0:T(8,128)(2,1)} %merge.8), channel_id=1, source_target_pairs={{0,112},{8,120},{16,0},{24,8},{32,16},{40,24},{48,32},{56,40},{64,... | collective-permute-start | bytes 663560 | tf_op jit(solution)/shard_map/ppermute | solution.py:335
  129.8 2.7 %collective-permute-done.12.first = bf16[96,1152]{1,0:T(8,128)(2,1)S(1)} collective-permute-done((bf16[96,1152]{1,0:T(8,128)(2,1)}, bf16[96,1152]{1,0:T(8,128)(2,1)S(1)}, u32[]{:S(2)}, u32[]{:S(2)}) %collective-permute-start.12) | collective-permute-done | bytes 221216 | tf_op jit(solution)/shard_map/ppermute | solution.py:332
  132.5 0.7 copy-done.5
  133.2 2.0 %merge.6 = bf16[96,1152]{1,0:T(8,128)(2,1)} custom-call(bf16[96,1152]{1,0:T(8,128)(2,1)} %copy-done.5, bf16[96,1152]{1,0:T(8,128)(2,1)} %get-tuple-element.43.second), custom_call_target="tpu_custom_call" | custom-call | flops 393216 | bytes 600000 | tf_op jit(solution)/shard_map/merge/pallas_call | solution.py:318
  135.2 0.0 collective-permute-start.13
  135.2 0.0 collective-permute-done.16.first
  135.2 0.7 copy-done.6
  135.9 2.0 %merge.9 = bf16[96,1152]{1,0:T(8,128)(2,1)} custom-call(bf16[96,1152]{1,0:T(8,128)(2,1)} %copy-done.6, bf16[96,1152]{1,0:T(8,128)(2,1)} %get-tuple-element.47.second), custom_call_target="tpu_custom_call" | custom-call | flops 393216 | bytes 600000 | tf_op jit(solution)/shard_map/merge/pallas_call | solution.py:318
  137.9 3.2 %collective-permute-start.17 = (bf16[96,1152]{1,0:T(8,128)(2,1)}, bf16[96,1152]{1,0:T(8,128)(2,1)S(1)}, u32[]{:S(2)}, u32[]{:S(2)}) collective-permute-start(bf16[96,1152]{1,0:T(8,128)(2,1)} %merge.9), channel_id=1, source_target_pairs={{0,112},{8,120},{16,0},{24,8},{32,16},{40,24},{48,32},{56,40},{64,... | collective-permute-start | bytes 663560 | tf_op jit(solution)/shard_map/ppermute | solution.py:335
  141.1 1.8 %collective-permute-done.13.first = bf16[96,1152]{1,0:T(8,128)(2,1)S(1)} collective-permute-done((bf16[96,1152]{1,0:T(8,128)(2,1)}, bf16[96,1152]{1,0:T(8,128)(2,1)S(1)}, u32[]{:S(2)}, u32[]{:S(2)}) %collective-permute-start.13) | collective-permute-done | bytes 221216 | tf_op jit(solution)/shard_map/ppermute | solution.py:332
  143.0 0.7 copy-done.7
  143.6 2.0 %merge.7 = bf16[96,1152]{1,0:T(8,128)(2,1)} custom-call(bf16[96,1152]{1,0:T(8,128)(2,1)} %copy-done.7, bf16[96,1152]{1,0:T(8,128)(2,1)} %get-tuple-element.44.second), custom_call_target="tpu_custom_call" | custom-call | flops 393216 | bytes 600000 | tf_op jit(solution)/shard_map/merge/pallas_call | solution.py:318
  145.6 0.0 collective-permute-start.14
  146.3 4.5 %queue.1 = bf16[768,1024]{1,0:T(8,128)(2,1)} custom-call(s32[1]{0:T(128)S(6)} %select_n.46.shift, bf16[768,1024]{1,0:T(8,128)(2,1)} %keys.1, bf16[768,1024]{1,0:T(8,128)(2,1)} %fresh.1), custom_call_target="tpu_custom_call" | custom-call | flops 1207959552 | bytes 5000000 | tf_op jit(solution)/shard_map/queue/pallas_call | solution.py:356
  150.8 0.0 collective-permute-done.17.second
  150.8 2.2 %collective-permute-done.14.first = bf16[96,1152]{1,0:T(8,128)(2,1)S(1)} collective-permute-done((bf16[96,1152]{1,0:T(8,128)(2,1)}, bf16[96,1152]{1,0:T(8,128)(2,1)S(1)}, u32[]{:S(2)}, u32[]{:S(2)}) %collective-permute-start.14) | collective-permute-done | bytes 221216 | tf_op jit(solution)/shard_map/ppermute | solution.py:332
  153.0 0.7 copy-done.2
  153.7 4.1 %final.1 = (bf16[96,1024]{1,0:T(8,128)(2,1)}, f32[96,1]{1,0:T(8,128)}) custom-call(bf16[96,1152]{1,0:T(8,128)(2,1)} %copy-done.2, bf16[96,1152]{1,0:T(8,128)(2,1)} %copy-done.1, bf16[96,1152]{1,0:T(8,128)(2,1)} %get-tuple-element.48.own, f32[96,1024]{1,0:T(8,128)} %get-tuple-element.49.hidden, f32[1,1024]{1,0:T(1,128)} %bitcast.13, ...), custom_call_target="tpu_custom_call" | custom-call | flops 201326592 | bytes 3500000 | tf_op jit(solution)/shard_map/final/pallas_call | solution.py:339
  157.8 1.4 reduce
  (30 shorter events, 0.1 us)
Async XLA Ops:
  7.2 1.0 copy-start
  7.2 50.4 %all-gather.2.cloned.1.call-start = ((), (), s32[]{:S(2)}) async-start(), calls=%async_computation.1 | async-start | bytes 1179648 | tf_op jit(solution)/shard_map/all_gather | solution.py:258
  9.7 55.2 %copy-start.3 = (bf16[96,1152]{1,0:T(8,128)(2,1)}, bf16[96,1152]{1,0:T(8,128)(2,1)S(1)}, u32[]{:S(2)}) copy-start(bf16[96,1152]{1,0:T(8,128)(2,1)S(1)} %fusion.1.refs_0_) | copy-start | bytes 663556
  9.8 143.2 %reduce-scatter.2.cloned.1.call-start = ((), (), s32[]{:S(2)}) async-start(), calls=%async_computation.2 | async-start | bytes 1769472 | tf_op jit(solution)/shard_map/reduce_scatter | solution.py:283
  9.8 47.8 %collective-permute-start.6 = (bf16[768,1024]{1,0:T(8,128)(2,1)}, bf16[768,1024]{1,0:T(8,128)(2,1)S(1)}, u32[]{:S(2)}, u32[]{:S(2)}) collective-permute-start(bf16[768,1024]{1,0:T(8,128)(2,1)} %keys.1), channel_id=1, source_target_pairs={{0,128},{8,136},{16,144},{24,152},{32,160},{40,168},{48,176},{56,1... | collective-permute-start | bytes 4718600 | tf_op jit(solution)/shard_map/ppermute | solution.py:241
  12.1 9.3 %collective-permute-start = (bf16[96,1152]{1,0:T(8,128)(2,1)S(1)}, bf16[96,1152]{1,0:T(8,128)(2,1)S(1)}, u32[]{:S(2)}, u32[]{:S(2)}) collective-permute-start(bf16[96,1152]{1,0:T(8,128)(2,1)S(1)} %fusion.1.refs_0_), channel_id=1, source_target_pairs={{0,16},{8,24},{16,32},{24,40},{32,48},{40,56},{48,64},{56,72},{64,... | collective-permute-start | bytes 663560 | tf_op jit(solution)/shard_map/ppermute | solution.py:254
  12.3 9.1 %collective-permute-start.1 = (bf16[96,1152]{1,0:T(8,128)(2,1)S(1)}, bf16[96,1152]{1,0:T(8,128)(2,1)S(1)}, u32[]{:S(2)}, u32[]{:S(2)}) collective-permute-start(bf16[96,1152]{1,0:T(8,128)(2,1)S(1)} %fusion.1.refs_0_), channel_id=1, source_target_pairs={{0,112},{8,120},{16,0},{24,8},{32,16},{40,24},{48,32},{56,40},{64,... | collective-permute-start | bytes 663560 | tf_op jit(solution)/shard_map/ppermute | solution.py:256
  21.4 43.6 %copy-start.11 = (bf16[96,1152]{1,0:T(8,128)(2,1)}, bf16[96,1152]{1,0:T(8,128)(2,1)S(1)}, u32[]{:S(2)}) copy-start(bf16[96,1152]{1,0:T(8,128)(2,1)S(1)} %collective-permute-done.refs_1_) | copy-start | bytes 663556
  21.4 43.6 %copy-start.12 = (bf16[96,1152]{1,0:T(8,128)(2,1)}, bf16[96,1152]{1,0:T(8,128)(2,1)S(1)}, u32[]{:S(2)}) copy-start(bf16[96,1152]{1,0:T(8,128)(2,1)S(1)} %collective-permute-done.1.refs_2_) | copy-start | bytes 663556
  21.4 7.6 %collective-permute-start.2 = (bf16[96,1152]{1,0:T(8,128)(2,1)S(1)}, bf16[96,1152]{1,0:T(8,128)(2,1)S(1)}, u32[]{:S(2)}, u32[]{:S(2)}) collective-permute-start(bf16[96,1152]{1,0:T(8,128)(2,1)S(1)} %collective-permute-done.refs_1_), channel_id=1, source_target_pairs={{0,16},{8,24},{16,32},{24,40},{32,48},{40,56},{48,64},{56,72},{64,... | collective-permute-start | bytes 663560 | tf_op jit(solution)/shard_map/ppermute | solution.py:254
  21.5 7.5 %collective-permute-start.3 = (bf16[96,1152]{1,0:T(8,128)(2,1)S(1)}, bf16[96,1152]{1,0:T(8,128)(2,1)S(1)}, u32[]{:S(2)}, u32[]{:S(2)}) collective-permute-start(bf16[96,1152]{1,0:T(8,128)(2,1)S(1)} %collective-permute-done.1.refs_2_), channel_id=1, source_target_pairs={{0,112},{8,120},{16,0},{24,8},{32,16},{40,24},{48,32},{56,40},{64,... | collective-permute-start | bytes 663560 | tf_op jit(solution)/shard_map/ppermute | solution.py:256
  29.0 28.6 %copy-start.13 = (bf16[96,1152]{1,0:T(8,128)(2,1)}, bf16[96,1152]{1,0:T(8,128)(2,1)S(1)}, u32[]{:S(2)}) copy-start(bf16[96,1152]{1,0:T(8,128)(2,1)S(1)} %collective-permute-done.2.refs_3_) | copy-start | bytes 663556
  29.0 28.6 %copy-start.14 = (bf16[96,1152]{1,0:T(8,128)(2,1)}, bf16[96,1152]{1,0:T(8,128)(2,1)S(1)}, u32[]{:S(2)}) copy-start(bf16[96,1152]{1,0:T(8,128)(2,1)S(1)} %collective-permute-done.3.refs_4_) | copy-start | bytes 663556
  29.0 7.2 %collective-permute-start.4 = (bf16[96,1152]{1,0:T(8,128)(2,1)S(1)}, bf16[96,1152]{1,0:T(8,128)(2,1)S(1)}, u32[]{:S(2)}, u32[]{:S(2)}) collective-permute-start(bf16[96,1152]{1,0:T(8,128)(2,1)S(1)} %collective-permute-done.2.refs_3_), channel_id=1, source_target_pairs={{0,16},{8,24},{16,32},{24,40},{32,48},{40,56},{48,64},{56,72},{64,... | collective-permute-start | bytes 663560 | tf_op jit(solution)/shard_map/ppermute | solution.py:254
  31.0 5.9 %collective-permute-start.5 = (bf16[96,1152]{1,0:T(8,128)(2,1)S(1)}, bf16[96,1152]{1,0:T(8,128)(2,1)S(1)}, u32[]{:S(2)}, u32[]{:S(2)}) collective-permute-start(bf16[96,1152]{1,0:T(8,128)(2,1)S(1)} %collective-permute-done.3.refs_4_), channel_id=1, source_target_pairs={{0,112},{8,120},{16,0},{24,8},{32,16},{40,24},{48,32},{56,40},{64,... | collective-permute-start | bytes 663560 | tf_op jit(solution)/shard_map/ppermute | solution.py:256
  36.2 21.4 %copy-start.15 = (bf16[96,1152]{1,0:T(8,128)(2,1)}, bf16[96,1152]{1,0:T(8,128)(2,1)S(1)}, u32[]{:S(2)}) copy-start(bf16[96,1152]{1,0:T(8,128)(2,1)S(1)} %collective-permute-done.4.refs_5_) | copy-start | bytes 663556
  37.0 20.7 %copy-start.16 = (bf16[96,1152]{1,0:T(8,128)(2,1)}, bf16[96,1152]{1,0:T(8,128)(2,1)S(1)}, u32[]{:S(2)}) copy-start(bf16[96,1152]{1,0:T(8,128)(2,1)S(1)} %collective-permute-done.5.refs_6_) | copy-start | bytes 663556
  37.0 7.1 %collective-permute-start.7 = (bf16[96,1152]{1,0:T(8,128)(2,1)S(1)}, bf16[96,1152]{1,0:T(8,128)(2,1)S(1)}, u32[]{:S(2)}, u32[]{:S(2)}) collective-permute-start(bf16[96,1152]{1,0:T(8,128)(2,1)S(1)} %collective-permute-done.4.refs_5_), channel_id=1, source_target_pairs={{0,16},{8,24},{16,32},{24,40},{32,48},{40,56},{48,64},{56,72},{64,... | collective-permute-start | bytes 663560 | tf_op jit(solution)/shard_map/ppermute | solution.py:254
  44.1 0.7 copy-start.17
  57.6 7.4 %copy-start.9 = (bf16[768,1024]{1,0:T(8,128)(2,1)}, bf16[768,1024]{1,0:T(8,128)(2,1)S(1)}, u32[]{:S(2)}) copy-start(bf16[768,1024]{1,0:T(8,128)(2,1)S(1)} %collective-permute-done.6.refs_13_.refs_10_) | copy-start | bytes 4718596
  57.6 7.4 %collective-permute-start.8 = (bf16[768,1024]{1,0:T(8,128)(2,1)S(1)}, bf16[768,1024]{1,0:T(8,128)(2,1)}, u32[]{:S(2)}, u32[]{:S(2)}) collective-permute-start(bf16[768,1024]{1,0:T(8,128)(2,1)S(1)} %collective-permute-done.6.refs_13_.refs_10_), channel_id=1, source_target_pairs={{0,8},{8,0},{16,24},{24,16},{32,40},{40,32},{48,56},{56,48},{64,72... | collective-permute-start | bytes 4718600 | tf_op jit(solution)/shard_map/ppermute | solution.py:260
  57.6 7.3 %collective-permute-start.10 = (bf16[768,1024]{1,0:T(8,128)(2,1)}, bf16[768,1024]{1,0:T(8,128)(2,1)}, u32[]{:S(2)}, u32[]{:S(2)}) collective-permute-start(bf16[768,1024]{1,0:T(8,128)(2,1)} %keys.1), channel_id=1, source_target_pairs={{0,8},{8,0},{16,24},{24,16},{32,40},{40,32},{48,56},{56,48},{64,72... | collective-permute-start | bytes 4718600 | tf_op jit(solution)/shard_map/ppermute | solution.py:242
  58.2 6.8 %collective-permute-start.9 = (bf16[4096,128]{1,0:T(8,128)(2,1)}, bf16[4096,128]{1,0:T(8,128)(2,1)S(1)}, u32[]{:S(2)}, u32[]{:S(2)}) collective-permute-start(bf16[4096,128]{1,0:T(8,128)(2,1)} %all-gather.2.cloned.1.call-done.refs_8_), channel_id=1, source_target_pairs={{0,8},{8,0},{16,24},{24,16},{32,40},{40,32},{48,56},{56,48},{64,72... | collective-permute-start | bytes 3145736 | tf_op jit(solution)/shard_map/ppermute | solution.py:261
  65.0 12.0 %copy-start.10 = (bf16[4096,128]{1,0:T(8,128)(2,1)}, bf16[4096,128]{1,0:T(8,128)(2,1)S(1)}, u32[]{:S(2)}) copy-start(bf16[4096,128]{1,0:T(8,128)(2,1)S(1)} %collective-permute-done.9.refs_9_) | copy-start | bytes 3145732
  107.2 14.0 %collective-permute-start.11 = (bf16[96,1152]{1,0:T(8,128)(2,1)}, bf16[96,1152]{1,0:T(8,128)(2,1)S(1)}, u32[]{:S(2)}, u32[]{:S(2)}) collective-permute-start(bf16[96,1152]{1,0:T(8,128)(2,1)} %get-tuple-element.41), channel_id=1, source_target_pairs={{0,16},{8,24},{16,32},{24,40},{32,48},{40,56},{48,64},{56,72},{64,... | collective-permute-start | bytes 663560 | tf_op jit(solution)/shard_map/ppermute | solution.py:332
  109.3 14.7 %collective-permute-start.15 = (bf16[96,1152]{1,0:T(8,128)(2,1)}, bf16[96,1152]{1,0:T(8,128)(2,1)S(1)}, u32[]{:S(2)}, u32[]{:S(2)}) collective-permute-start(bf16[96,1152]{1,0:T(8,128)(2,1)} %get-tuple-element.45), channel_id=1, source_target_pairs={{0,112},{8,120},{16,0},{24,8},{32,16},{40,24},{48,32},{56,40},{64,... | collective-permute-start | bytes 663560 | tf_op jit(solution)/shard_map/ppermute | solution.py:335
  121.2 0.7 copy-start.8
  123.9 8.6 %collective-permute-start.12 = (bf16[96,1152]{1,0:T(8,128)(2,1)}, bf16[96,1152]{1,0:T(8,128)(2,1)S(1)}, u32[]{:S(2)}, u32[]{:S(2)}) collective-permute-start(bf16[96,1152]{1,0:T(8,128)(2,1)} %merge.5), channel_id=1, source_target_pairs={{0,16},{8,24},{16,32},{24,40},{32,48},{40,56},{48,64},{56,72},{64,... | collective-permute-start | bytes 663560 | tf_op jit(solution)/shard_map/ppermute | solution.py:332
  123.9 0.7 copy-start.4
  126.6 8.6 %collective-permute-start.16 = (bf16[96,1152]{1,0:T(8,128)(2,1)}, bf16[96,1152]{1,0:T(8,128)(2,1)S(1)}, u32[]{:S(2)}, u32[]{:S(2)}) collective-permute-start(bf16[96,1152]{1,0:T(8,128)(2,1)} %merge.8), channel_id=1, source_target_pairs={{0,112},{8,120},{16,0},{24,8},{32,16},{40,24},{48,32},{56,40},{64,... | collective-permute-start | bytes 663560 | tf_op jit(solution)/shard_map/ppermute | solution.py:335
  132.5 0.7 copy-start.5
  135.2 7.8 %collective-permute-start.13 = (bf16[96,1152]{1,0:T(8,128)(2,1)}, bf16[96,1152]{1,0:T(8,128)(2,1)S(1)}, u32[]{:S(2)}, u32[]{:S(2)}) collective-permute-start(bf16[96,1152]{1,0:T(8,128)(2,1)} %merge.6), channel_id=1, source_target_pairs={{0,16},{8,24},{16,32},{24,40},{32,48},{40,56},{48,64},{56,72},{64,... | collective-permute-start | bytes 663560 | tf_op jit(solution)/shard_map/ppermute | solution.py:332
  135.2 0.7 copy-start.6
  137.9 12.9 %collective-permute-start.17 = (bf16[96,1152]{1,0:T(8,128)(2,1)}, bf16[96,1152]{1,0:T(8,128)(2,1)S(1)}, u32[]{:S(2)}, u32[]{:S(2)}) collective-permute-start(bf16[96,1152]{1,0:T(8,128)(2,1)} %merge.9), channel_id=1, source_target_pairs={{0,112},{8,120},{16,0},{24,8},{32,16},{40,24},{48,32},{56,40},{64,... | collective-permute-start | bytes 663560 | tf_op jit(solution)/shard_map/ppermute | solution.py:335
  143.0 0.7 copy-start.7
  145.6 7.4 %collective-permute-start.14 = (bf16[96,1152]{1,0:T(8,128)(2,1)}, bf16[96,1152]{1,0:T(8,128)(2,1)S(1)}, u32[]{:S(2)}, u32[]{:S(2)}) collective-permute-start(bf16[96,1152]{1,0:T(8,128)(2,1)} %merge.7), channel_id=1, source_target_pairs={{0,16},{8,24},{16,32},{24,40},{32,48},{40,56},{48,64},{56,72},{64,... | collective-permute-start | bytes 663560 | tf_op jit(solution)/shard_map/ppermute | solution.py:332
  150.8 2.2 %copy-start.1 = (bf16[96,1152]{1,0:T(8,128)(2,1)}, bf16[96,1152]{1,0:T(8,128)(2,1)S(1)}, u32[]{:S(2)}) copy-start(bf16[96,1152]{1,0:T(8,128)(2,1)S(1)} %collective-permute-done.17.second) | copy-start | bytes 663556
  153.0 0.7 copy-start.2
Sparse Core Ops, SparseCore 0:
  10.4 44.7 all-gather.1
  77.1 44.9 reduce-scatter.1
